TPU v7x, 512 devices: a whole 4x8x8 slice. The times are simulated.
512 devices in a mesh: bulk: 32 (over x, y), group: 16 (over z, core).
Axes of the slice: x: 4, y: 8, z: 8, core: 2. Of those that a mesh axis runs over, the one named last changes fastest.
Arguments:
- rhs: bfloat16 [64, 256, 64, 64], P('bulk', 'group'), may hold values from -40 to 40
- diag_blocks: bfloat16 [64, 256, 64, 64], P('bulk', 'group'), may hold values from -0.4 to 2
- precond_blocks: bfloat16 [64, 256, 64, 64], P('bulk', 'group'), may hold values from -0.15 to 0.7
- coupling: float32 [64, 256, 256], P('bulk', 'group'), may hold values from 0.05 to 1.2
- face_open: int32 [64, 256, 4], P('bulk', 'group'), may hold values 0 or 1
- agg_id: int32 [64, 256], P('bulk', 'group'), may hold values from 0 to 3
- coarse_basis: float32 [64, 8], replicated, may hold values from -0.75 to 0.75
- coarse_inv: float32 [32, 512, 512], P('bulk', None, 'group'), may hold values from -1 to 2, as said below
Outputs:
- adjoint: bfloat16 [64, 256, 64, 64], P('bulk', 'group')
Inputs may be any that keep to these rules, and one draw needn't show every extreme that they name: coarse_inv[b] is symmetric for every b.
All inputs are finite; a program needn't handle non-finite values. No bound on the sum of `face_open` on one device may be relied on, other than what follows from the above.
Results may differ from a plain program's by a relative error of at most 0.012.
Values may be sent and summed in bfloat16 or wider, within the bound.
A program may use at most 64 MiB of HBM per device.

v0:
```python
import jax
import jax.numpy as jnp
from jax import lax
from jax.sharding import PartitionSpec as P

NS = 64
COLS = 64
CX = 2
CY = 16
AGGS = 4
COMPS = 8
ITERS = 3


tiny_eps = 1e-06


def padded_2(cells, sides, width):
    for axis, dim in sides:
        count = lax.axis_size(axis)
        ends = count - 1
        head = lax.slice_in_dim(cells, 0, width, axis=dim)
        tail = lax.slice_in_dim(cells, cells.shape[dim] - width, cells.shape[dim], axis=dim)
        cells = jnp.concatenate(
            [
                lax.ppermute(tail, axis, [(i, (i + 1) % count) for i in range(ends)]),
                cells,
                lax.ppermute(head, axis, [((i + 1) % count, i) for i in range(ends)]),
            ],
            axis=dim,
        )
    return cells


def givens_solve(hessen_cols, beta_norm):
    cosine_list = []
    sine_list = []
    target = [beta_norm] + [jnp.zeros_like(beta_norm) for _ in range(ITERS)]
    triangle = []
    for section in range(ITERS):
        column = list(hessen_cols[section])
        for earlier in range(section):
            upper = column[earlier]
            lower = column[earlier + 1]
            column[earlier] = cosine_list[earlier] * upper + sine_list[earlier] * lower
            column[earlier + 1] = -sine_list[earlier] * upper + cosine_list[earlier] * lower
        upper = column[section]
        lower = column[section + 1]
        radius = jnp.sqrt(upper * upper + lower * lower)
        cosine = upper / radius
        sine_val = lower / radius
        cosine_list.append(cosine)
        sine_list.append(sine_val)
        column[section] = radius
        carried = target[section]
        target[section] = cosine * carried
        target[section + 1] = -sine_val * carried
        triangle.append(column[: section + 1])
    solution = [None] * ITERS
    for section in reversed(range(ITERS)):
        accumulated = target[section]
        for later in range(section + 1, ITERS):
            accumulated = accumulated - triangle[later][section] * solution[later]
        solution[section] = accumulated / triangle[section][section]
    return solution


def body(rhs, diag_blocks, precond_blocks, coupling, face_open, agg_id, coarse_basis, coarse_inv):
    highest = lax.Precision.HIGHEST
    cells = CX * CY
    coarse_rows_dev = AGGS * COMPS
    coeff = coupling.reshape(CX, CY, 4, NS) * face_open.astype(jnp.float32)[..., None]
    one_hot = (agg_id.reshape(cells, 1) == jnp.arange(AGGS, dtype=jnp.int32)[None, :]).astype(
        jnp.float32
    )
    weight_scale = (AGGS / (CX * CY)) ** 0.5
    inverse_cols = coarse_inv[0]
    start = rhs.astype(jnp.float32)
    start_local = jnp.sum(start * start, axis=(0, 1, 2))
    beta_norm = None
    inv_beta = None
    start_sq = lax.psum(start_local, ("bulk", "group"))
    beta_norm = jnp.sqrt(start_sq + tiny_eps)
    inv_beta = 1.0 / beta_norm
    krylov = [start]
    precond_vecs = []
    hessen_cols = []
    for section in range(ITERS):
        precondition_vector = krylov[section]
        rounded = precondition_vector.astype(jnp.bfloat16)
        local = jnp.einsum(
            "xyij,xyjr->xyir", precond_blocks, rounded, preferred_element_type=jnp.float32
        )
        summed = jnp.dot(
            one_hot.T, precondition_vector.reshape(cells, NS * COLS), precision=highest
        )
        residual = jnp.einsum(
            "kjr,jc->kcr", summed.reshape(AGGS, NS, COLS), coarse_basis, precision=highest
        )
        residual = (residual * weight_scale).reshape(coarse_rows_dev, COLS)
        correct = lax.psum_scatter(
            jnp.dot(inverse_cols, residual, precision=highest),
            "group",
            scatter_dimension=0,
            tiled=True,
        )
        spread = jnp.einsum(
            "jc,kcr->kjr", coarse_basis, correct.reshape(AGGS, COMPS, COLS), precision=highest
        )
        back = jnp.dot(one_hot, spread.reshape(AGGS, NS * COLS), precision=highest)
        zvec = (local + back.reshape(CX, CY, NS, COLS)).astype(jnp.bfloat16)
        precond_vecs.append(zvec)
        padded = padded_2(zvec, (("bulk", 0), ("group", 1)), 1)
        own = jnp.einsum("xyij,xyir->xyjr", diag_blocks, zvec, preferred_element_type=jnp.float32)
        near = coeff[:, :, 0, :, None] * padded[:-2, 1:-1].astype(jnp.float32)
        near = near + coeff[:, :, 1, :, None] * padded[2:, 1:-1].astype(jnp.float32)
        near = near + coeff[:, :, 2, :, None] * padded[1:-1, :-2].astype(jnp.float32)
        near = near + coeff[:, :, 3, :, None] * padded[1:-1, 2:].astype(jnp.float32)
        image = own - near
        rows = [jnp.sum(vector * image, axis=(0, 1, 2)) for vector in krylov]
        local_dots = jnp.stack(rows)
        summed = lax.psum(local_dots, ("bulk", "group"))
        factors = [inv_beta] + [jnp.ones_like(inv_beta) for _ in range(section)]
        scale_now = factors[section]
        projected = [summed[i] * factors[i] * scale_now for i in range(section + 1)]
        image = image * scale_now
        for earlier in range(section + 1):
            image = image - projected[earlier] * (krylov[earlier] * factors[earlier])
        squared = lax.psum(jnp.sum(image * image, axis=(0, 1, 2)), ("bulk", "group"))
        next_norm = jnp.sqrt(squared + tiny_eps)
        hessen_cols.append(projected + [next_norm])
        if section + 1 < ITERS:
            krylov.append(image / next_norm)
    solution = givens_solve(hessen_cols, beta_norm)
    total = jnp.zeros(rhs.shape, jnp.float32)
    for section in range(ITERS):
        factor_now = inv_beta if section == 0 else jnp.ones_like(inv_beta)
        total = total + solution[section] * factor_now * precond_vecs[section].astype(jnp.float32)
    return total.astype(jnp.bfloat16)


def solution(mesh):
    in_specs = (
        P("bulk", "group", None, None),
        P("bulk", "group", None, None),
        P("bulk", "group", None, None),
        P("bulk", "group", None),
        P("bulk", "group", None),
        P("bulk", "group"),
        P(),
        P("bulk", None, "group"),
    )
    out_specs = P("bulk", "group", None, None)
    return jax.shard_map(body, mesh=mesh, in_specs=in_specs, out_specs=out_specs, check_vma=False)
```

profile of v0, /device:TPU:1, one launch (start us, length us, event | category | flops | bytes accessed | tf_op | source)
XLA Modules:
  0.0 879.1 jit_solution(18435156557588775066)
XLA Ops:
  7.4 1.5 reshape.115
  11.2 0.8 copy.84
  13.0 61.4 %reduce-scatter.10.cloned.1.call-done = f32[32,64]{1,0:T(8,128)} async-done(((f32[512,64]{1,0:T(8,128)}), f32[32,64]{1,0:T(8,128)}) %reduce-scatter.10.cloned.1.call-update) | async-done | bytes 8208 | tf_op jit(solution)/shard_map/reduce_scatter | solution.py:101
  74.3 1.1 convolution_bitcast_fusion.9
  78.1 3.2 collective-permute-start
  81.3 1.3 collective-permute-start.1
  82.6 1.9 collective-permute-done
  84.5 3.8 collective-permute-done.1
  88.4 5.2 collective-permute-start.2
  93.6 2.9 collective-permute-start.3
  96.5 2.7 collective-permute-done.3
  99.2 2.8 fusion.19
  102.0 101.8 %all-reduce = (f32[64]{0:T(128)S(1)}, f32[64]{0:T(128)S(1)}) all-reduce(f32[64]{0:T(128)S(1)} %get-tuple-element.11, f32[64]{0:T(128)S(1)} %get-tuple-element.10), channel_id=1, replica_groups=mesh['bulk'=32,'group'=16] {'bulk','group'}, use_global_device_ids=true, to_apply=%region_4.0 | all-reduce | flops 128 | bytes 1024 | tf_op jit(solution)/shard_map/psum | solution.py:82
  204.3 1.5 multiply_reduce_fusion.4
  205.9 94.5 %psum.51 = f32[64]{0:T(128)S(1)} all-reduce(f32[64]{0:T(128)S(1)} %multiply_reduce_fusion.4), channel_id=1, replica_groups=mesh['bulk'=32,'group'=16] {'bulk','group'}, use_global_device_ids=true, to_apply=%region_6.0 | all-reduce | flops 64 | bytes 512 | tf_op jit(solution)/shard_map/psum | solution.py:129
  300.9 1.4 fusion.27
  302.7 1.4 dot_general.119
  304.1 2.2 fusion.25
  307.8 53.0 %reduce-scatter.12.cloned.1.call-done = f32[32,64]{1,0:T(8,128)} async-done(((f32[512,64]{1,0:T(8,128)}), f32[32,64]{1,0:T(8,128)}) %reduce-scatter.12.cloned.1.call-update) | async-done | bytes 8208 | tf_op jit(solution)/shard_map/reduce_scatter | solution.py:101
  360.8 1.1 convolution_bitcast_fusion.7
  363.5 3.2 collective-permute-start.4
  366.7 1.3 collective-permute-start.5
  368.0 2.0 collective-permute-done.4
  369.9 3.8 collective-permute-done.5
  373.8 5.4 collective-permute-start.6
  379.2 2.9 collective-permute-start.7
  382.2 2.6 collective-permute-done.7
  384.8 1.4 fusion.21
  386.2 101.5 %psum.52 = f32[2,64]{1,0:T(2,128)S(1)} all-reduce(f32[2,64]{1,0:T(2,128)S(1)} %pad_maximum_fusion.34), channel_id=1, replica_groups=mesh['bulk'=32,'group'=16] {'bulk','group'}, use_global_device_ids=true, to_apply=%region_10.0 | all-reduce | flops 128 | bytes 1024 | tf_op jit(solution)/shard_map/psum | solution.py:122
  488.3 94.6 %psum.53 = f32[64]{0:T(128)S(1)} all-reduce(f32[64]{0:T(128)S(1)} %multiply_reduce_fusion.2), channel_id=1, replica_groups=mesh['bulk'=32,'group'=16] {'bulk','group'}, use_global_device_ids=true, to_apply=%region_12.0 | all-reduce | flops 64 | bytes 512 | tf_op jit(solution)/shard_map/psum | solution.py:129
  583.3 1.5 broadcast_divide_fusion
  584.8 1.2 reshape.124
  586.0 2.5 dot_general.133
  588.5 2.2 fusion.23
  592.0 52.9 %reduce-scatter.14.cloned.1.call-done = f32[32,64]{1,0:T(8,128)} async-done(((f32[512,64]{1,0:T(8,128)}), f32[32,64]{1,0:T(8,128)}) %reduce-scatter.14.cloned.1.call-update) | async-done | bytes 8208 | tf_op jit(solution)/shard_map/reduce_scatter | solution.py:101
  645.0 1.1 convolution_bitcast_fusion.5
  648.0 3.1 collective-permute-start.8
  651.1 1.3 collective-permute-start.9
  652.4 2.0 collective-permute-done.8
  654.4 3.8 collective-permute-done.9
  658.3 5.4 collective-permute-start.10
  663.7 2.7 collective-permute-start.11
  666.4 2.9 collective-permute-done.11
  669.3 2.8 fusion.22
  672.1 101.7 %psum.54 = f32[3,64]{1,0:T(4,128)S(1)} all-reduce(f32[3,64]{1,0:T(4,128)S(1)} %pad_maximum_fusion.33), channel_id=1, replica_groups=mesh['bulk'=32,'group'=16] {'bulk','group'}, use_global_device_ids=true, to_apply=%region_17.0 | all-reduce | flops 192 | bytes 1536 | tf_op jit(solution)/shard_map/psum | solution.py:122
  773.8 1.6 fusion.18
  775.5 94.5 %psum.55 = f32[64]{0:T(128)S(1)} all-reduce(f32[64]{0:T(128)S(1)} %fusion.18), channel_id=1, replica_groups=mesh['bulk'=32,'group'=16] {'bulk','group'}, use_global_device_ids=true, to_apply=%region_19.0 | all-reduce | flops 64 | bytes 512 | tf_op jit(solution)/shard_map/psum | solution.py:129
  870.1 2.5 add_convert_fusion
  (100 shorter events, 15.6 us)
Async XLA Ops:
  6.5 92.7 %copy-start = (bf16[2,16,64,64]{3,2,1,0:T(8,128)(2,1)S(1)}, bf16[2,16,64,64]{3,2,1,0:T(8,128)(2,1)}, u32[]{:S(2)}) copy-start(bf16[2,16,64,64]{3,2,1,0:T(8,128)(2,1)} %param.9) | copy-start | bytes 786436
  6.5 67.8 %reduce-scatter.10.cloned.1.call-start = ((), (), s32[]{:S(2)}) async-start(), calls=%async_computation.3 | async-start | bytes 278528 | tf_op jit(solution)/shard_map/reduce_scatter | solution.py:101
  9.4 0.7 copy-start.9
  10.1 0.8 copy-start.8
  12.1 0.7 copy-start.12
  12.1 0.8 copy-start.10
  12.1 348.6 %reduce-scatter.12.cloned.1.call-start = ((), (), s32[]{:S(2)}) async-start(), calls=%async_computation.4 | async-start | bytes 278528 | tf_op jit(solution)/shard_map/reduce_scatter | solution.py:101
  75.7 0.7 copy-start.11
  76.4 1.0 copy-start.1
  76.4 1.2 copy-start.5
  78.0 21.2 %copy-start.2 = (bf16[2,16,64,64]{3,2,1,0:T(8,128)(2,1)}, bf16[2,16,64,64]{3,2,1,0:T(8,128)(2,1)S(1)}, u32[]{:S(2)}) copy-start(bf16[2,16,64,64]{3,2,1,0:T(8,128)(2,1)S(1)} %fusion.5) | copy-start | bytes 786436
  78.1 6.4 collective-permute-start
  81.3 7.1 collective-permute-start.1
  88.4 8.1 collective-permute-start.2
  93.6 5.6 collective-permute-start.3
  203.8 0.5 copy-start.15
  300.4 0.5 copy-start.17
  307.7 337.3 %reduce-scatter.14.cloned.1.call-start = ((), (), s32[]{:S(2)}) async-start(), calls=%async_computation.5 | async-start | bytes 278528 | tf_op jit(solution)/shard_map/reduce_scatter | solution.py:101
  363.4 21.4 %copy-start.3 = (bf16[2,16,64,64]{3,2,1,0:T(8,128)(2,1)}, bf16[2,16,64,64]{3,2,1,0:T(8,128)(2,1)S(1)}, u32[]{:S(2)}) copy-start(bf16[2,16,64,64]{3,2,1,0:T(8,128)(2,1)S(1)} %fusion.6) | copy-start | bytes 786436
  363.5 6.5 collective-permute-start.4
  366.7 7.1 collective-permute-start.5
  373.8 8.3 collective-permute-start.6
  379.2 5.6 collective-permute-start.7
  386.2 101.8 %copy-start.7 = (f32[2,16,64,64]{3,2,1,0:T(8,128)}, f32[2,16,64,64]{3,2,1,0:T(8,128)S(1)}, u32[]{:S(2)}) copy-start(f32[2,16,64,64]{3,2,1,0:T(8,128)S(1)} %get-tuple-element.18) | copy-start | bytes 1572868
  487.7 0.6 copy-start.13
  582.9 0.5 copy-start.19
  646.4 1.0 copy-start.6
  648.0 21.3 %copy-start.4 = (bf16[2,16,64,64]{3,2,1,0:T(8,128)(2,1)}, bf16[2,16,64,64]{3,2,1,0:T(8,128)(2,1)S(1)}, u32[]{:S(2)}) copy-start(bf16[2,16,64,64]{3,2,1,0:T(8,128)(2,1)S(1)} %fusion.7) | copy-start | bytes 786436
  648.0 6.4 collective-permute-start.8
  651.1 7.1 collective-permute-start.9
  658.3 8.2 collective-permute-start.10
  663.7 5.6 collective-permute-start.11
  773.8 96.2 %copy-start.18 = (f32[64]{0:T(128)S(1)}, f32[64]{0:T(128)}, u32[]{:S(2)}) copy-start(f32[64]{0:T(128)} %copy-done.17) | copy-start | bytes 772
  773.8 96.2 %copy-start.20 = (f32[64]{0:T(128)S(1)}, f32[64]{0:T(128)}, u32[]{:S(2)}) copy-start(f32[64]{0:T(128)} %copy-done.19) | copy-start | bytes 772
  775.4 94.6 %copy-start.14 = (f32[2,64]{1,0:T(2,128)S(1)}, f32[2,64]{1,0:T(2,128)}, u32[]{:S(2)}) copy-start(f32[2,64]{1,0:T(2,128)} %copy-done.13) | copy-start | bytes 1540
  775.4 94.6 %copy-start.16 = (f32[64]{0:T(128)S(1)}, f32[64]{0:T(128)}, u32[]{:S(2)}) copy-start(f32[64]{0:T(128)} %copy-done.15) | copy-start | bytes 772
Sparse Core Ops, SparseCore 0:
  12.2 62.0 reduce-scatter.9
  307.8 52.8 reduce-scatter.11
  592.2 52.7 reduce-scatter.13
where the time goes:
time: 881 us; the launch traced here: 879 us
  blocking collectives  589 us (67%)
  waiting for transfers between devices  193 us (22%)
  starting transfers between devices  37.9 us (4%)
  matrix products  20.1 us (2%)
  local copies, waits for them, and re-layouts  16.8 us (2%)
  between operations  13.6 us (2%)
  other arithmetic  9.21 us (1%)
    psum x3, blocking collectives, body(): lax.psum(jnp.sum(image * image, axis=(0, 1, 2)), ('bulk', 'group'))  284 us
    psum x2, blocking collectives, body(): summed = lax.psum(local_dots, ('bulk', 'group'))  203 us
    reduce_scatter x3, waiting for transfers between devices, body(): lax.psum_scatter(jnp.dot(inverse_cols, residual, precision=highest), 'gro...  167 us
    psum x1, blocking collectives, body(): start_sq = lax.psum(start_local, ('bulk', 'group'))  102 us
    ppermute x6, starting transfers between devices, padded_2(): lax.ppermute(tail, axis, [(i, (i + 1) % count) for i in range(ends)])  25.5 us
    ppermute x6, waiting for transfers between devices, padded_2(): lax.ppermute(head, axis, [((i + 1) % count, i) for i in range(ends)])  19.7 us
  transfers between devices with their start and end apart: 15, of which 12 were waited for; matrix products, arithmetic and copies ran while one was open for 0% of the time, Pallas kernels for 0%

commit v1 on v0

v1 whole, which is shorter than its diff:
```python
import functools

import jax
import jax.numpy as jnp
from jax import lax
from jax.experimental import pallas as pl
from jax.experimental.pallas import tpu as pltpu
from jax.sharding import PartitionSpec as P

NS = 64
COLS = 64
CX = 2
CY = 16
AGGS = 4
COMPS = 8
ITERS = 3
HALF = CY // 2
PAIRS = CX * HALF
LANES = 2 * COLS

tiny_eps = 1e-06
f32 = jnp.float32
bf16 = jnp.bfloat16


def split_hi_lo(value):
    high = value.astype(bf16)
    low = (value - high.astype(f32)).astype(bf16)
    return high, low


def mm(left, right):
    return jnp.dot(left, right, preferred_element_type=f32)


def low_half(shape):
    return lax.broadcasted_iota(jnp.int32, shape, 1) < COLS


def givens_solve(hessen_cols, beta_norm):
    cosine_list = []
    sine_list = []
    target = [beta_norm] + [jnp.zeros_like(beta_norm) for _ in range(ITERS)]
    triangle = []
    for section in range(ITERS):
        column = list(hessen_cols[section])
        for earlier in range(section):
            upper = column[earlier]
            lower = column[earlier + 1]
            column[earlier] = cosine_list[earlier] * upper + sine_list[earlier] * lower
            column[earlier + 1] = -sine_list[earlier] * upper + cosine_list[earlier] * lower
        upper = column[section]
        lower = column[section + 1]
        radius = jnp.sqrt(upper * upper + lower * lower)
        cosine = upper / radius
        sine_val = lower / radius
        cosine_list.append(cosine)
        sine_list.append(sine_val)
        column[section] = radius
        carried = target[section]
        target[section] = cosine * carried
        target[section + 1] = -sine_val * carried
        triangle.append(column[: section + 1])
    result = [None] * ITERS
    for section in reversed(range(ITERS)):
        accumulated = target[section]
        for later in range(section + 1, ITERS):
            accumulated = accumulated - triangle[later][section] * result[later]
        result[section] = accumulated / triangle[section][section]
    return result


def kernel(
    nb,
    ng,
    rhs_hbm,
    diag_hbm,
    prec_hbm,
    coup_ref,
    face_ref,
    agg_ref,
    basis_ref,
    inv_hbm,
    out_ref,
    rhs_raw,
    prec,
    diag_raw,
    diag_t,
    inv_raw,
    inv_rows,
    coef,
    wtab,
    bas_t,
    bas_w,
    k0,
    k1,
    w0,
    w1,
    acc,
    local_y,
    zs,
    spread,
    res_send,
    res_buf,
    halo_x,
    halo_y,
    edge,
    sum_send,
    sum_group,
    tot_send,
    sum_bulk,
    load_sem,
    res_ssem,
    res_rsem,
    hx_ssem,
    hx_rsem,
    hy_ssem,
    hy_rsem,
    g_ssem,
    g_rsem,
    b_ssem,
    b_rsem,
):
    bulk = lax.axis_index("bulk")
    group = lax.axis_index("group")

    loads = [pltpu.make_async_copy(rhs_hbm, rhs_raw, load_sem.at[0])]
    prec_loads = []
    diag_loads = []
    for x in range(CX):
        for yh in range(2):
            n = x * 2 + yh
            src = (x, pl.ds(yh * HALF, HALF))
            dst = (pl.ds(x * HALF, HALF), pl.ds(yh * NS, NS))
            prec_loads.append(
                pltpu.make_async_copy(prec_hbm.at[src], prec.at[dst], load_sem.at[1 + n])
            )
            diag_loads.append(
                pltpu.make_async_copy(diag_hbm.at[src], diag_raw.at[dst], load_sem.at[5 + n])
            )
    inv_loads = [
        pltpu.make_async_copy(inv_hbm.at[:, kh], inv_raw.at[kh], load_sem.at[9 + kh])
        for kh in range(2)
    ]
    for copy in loads + prec_loads + inv_loads + diag_loads:
        copy.start()

    barrier = pltpu.get_barrier_semaphore()

    def greet_group(d, carry):
        pl.semaphore_signal(
            barrier,
            inc=1,
            device_id={"group": lax.rem(group + d, ng)},
            device_id_type=pl.DeviceIdType.MESH,
        )
        return carry

    def greet_bulk(d, carry):
        pl.semaphore_signal(
            barrier,
            inc=1,
            device_id={"bulk": lax.rem(bulk + d, nb)},
            device_id_type=pl.DeviceIdType.MESH,
        )
        return carry

    lax.fori_loop(1, ng, greet_group, 0)
    lax.fori_loop(1, nb, greet_bulk, 0)

    low8 = low_half((8, LANES))
    low64 = low_half((NS, LANES))

    def make_weights(p, carry):
        x = p // HALF
        yy = p % HALF
        first = agg_ref[x, yy]
        second = agg_ref[x, yy + HALF]
        for k in range(AGGS):
            wtab[p, k] = jnp.where(
                low8,
                jnp.where(first == k, 1.0, 0.0).astype(f32),
                jnp.where(second == k, 1.0, 0.0).astype(f32),
            )
        return carry

    lax.fori_loop(0, PAIRS, make_weights, 0)

    weight_scale = (AGGS / (CX * CY)) ** 0.5
    basis = basis_ref[...]
    turned = jnp.transpose(basis)
    high, low = split_hi_lo(turned)
    stacked = jnp.concatenate([high.astype(f32), high.astype(f32), low.astype(f32)], axis=0)
    bas_w[...] = jnp.transpose(stacked).astype(bf16)
    high, low = split_hi_lo(turned * weight_scale)
    bas_t[0] = jnp.concatenate([high, high], axis=0)
    bas_t[1] = jnp.concatenate([low, low], axis=0)

    loads[0].wait()

    def make_start(p, carry):
        x = p // HALF
        yy = p % HALF
        first = rhs_raw[x, yy].astype(f32)
        second = rhs_raw[x, yy + HALF].astype(f32)
        k0[p] = jnp.concatenate([first, second], axis=1)
        return carry

    lax.fori_loop(0, PAIRS, make_start, 0)

    def coarse_send(step, field):
        def add(p, sums):
            value = field[p].reshape(8, 8, LANES)
            return tuple(sums[k] + wtab[p, k] * value for k in range(AGGS))

        zero = jnp.zeros((8, 8, LANES), f32)
        sums = lax.fori_loop(0, PAIRS, add, (zero,) * AGGS)
        sums = [s.reshape(NS, LANES) for s in sums]
        parts = []
        for kl in range(2):
            keep = jnp.where(low64, sums[kl], sums[kl + 2])
            move = jnp.where(low64, sums[kl + 2], sums[kl])
            total = keep + pltpu.roll(move, COLS, 1)
            high, low = split_hi_lo(total)
            part = mm(bas_t[0], high) + mm(bas_t[0], low) + mm(bas_t[1], high)
            parts.append(part[:COMPS])
        res = jnp.concatenate(parts, axis=0).astype(bf16)
        res_send[step] = res
        res_buf[step, group] = res

        def push(d, carry):
            pltpu.make_async_remote_copy(
                src_ref=res_send.at[step],
                dst_ref=res_buf.at[step, group],
                send_sem=res_ssem.at[step],
                recv_sem=res_rsem.at[step],
                device_id={"group": lax.rem(group + d, ng)},
                device_id_type=pl.DeviceIdType.MESH,
            ).start()
            return carry

        lax.fori_loop(1, ng, push, 0)

    def all_but_one(buf, count, sem):
        return pltpu.make_async_copy(buf.at[pl.ds(0, count - 1)], buf.at[pl.ds(0, count - 1)], sem)

    def pair_product(mats, p, value):
        both = mm(mats[p], value)
        return jnp.where(low64, both[:NS], both[NS:])

    def local_part(field):
        def one(p, carry):
            local_y[p] = pair_product(prec, p, field[p].astype(bf16))
            return carry

        lax.fori_loop(0, PAIRS, one, 0)

    def halo_copies(step):
        left = lax.rem(bulk + nb - 1, nb)
        right = lax.rem(bulk + 1, nb)
        before = lax.rem(group + ng - 1, ng)
        after = lax.rem(group + 1, ng)
        copies = []
        for x, axis, target in ((0, "bulk", left), (1, "bulk", right)):
            copies.append(
                pltpu.make_async_remote_copy(
                    src_ref=zs.at[step, pl.ds(x * HALF, HALF)],
                    dst_ref=halo_x.at[step, 1 - x],
                    send_sem=hx_ssem.at[step, x],
                    recv_sem=hx_rsem.at[step, 1 - x],
                    device_id={axis: target},
                    device_id_type=pl.DeviceIdType.MESH,
                )
            )
        for x in range(CX):
            for side, row, target in ((0, HALF - 1, after), (1, 0, before)):
                copies.append(
                    pltpu.make_async_remote_copy(
                        src_ref=zs.at[step, x * HALF + row],
                        dst_ref=halo_y.at[step, x, side],
                        send_sem=hy_ssem.at[step, x, side],
                        recv_sem=hy_rsem.at[step, x, side],
                        device_id={"group": target},
                        device_id_type=pl.DeviceIdType.MESH,
                    )
                )
        return copies

    def finish_z(step):
        all_but_one(res_buf.at[step], ng, res_rsem.at[step]).wait()
        gathered = res_buf[step].reshape(ng * 16, LANES)
        both = mm(inv_rows[...], gathered)
        rows = AGGS * COMPS
        both = both[: 2 * rows] + both[2 * rows :]
        mixed = jnp.where(low_half((rows, LANES)), both[:rows], both[rows:])
        cor = mixed + pltpu.roll(mixed, COLS, 1)
        wide = jnp.concatenate([cor[k * COMPS : (k + 1) * COMPS] for k in range(AGGS)], axis=1)
        high, low = split_hi_lo(wide)
        wide = jnp.concatenate([high.astype(f32), low.astype(f32), high.astype(f32)], axis=0)
        wide = mm(bas_w[...], wide.astype(bf16))
        for k in range(AGGS):
            spread[k] = wide[:, k * LANES : (k + 1) * LANES]
        copies = halo_copies(step)

        def one(p, carry):
            x = p // HALF
            yy = p % HALF
            first = spread[agg_ref[x, yy]]
            second = spread[agg_ref[x, yy + HALF]]
            zs[step, p] = (local_y[p] + jnp.where(low64, first, second)).astype(bf16)
            return carry

        for x in range(CX):
            lax.fori_loop(x * HALF, (x + 1) * HALF, one, 0)
            copies[x].start()
            copies[2 + 2 * x].start()
            copies[3 + 2 * x].start()
        return copies

    def own_image(step):
        for x in range(CX):

            def one(yy, carry):
                p = x * HALF + yy
                own = pair_product(diag_t, p, zs[step, p])
                other = zs[step, (1 - x) * HALF + yy].astype(f32)
                acc[p] = own - coef[p, 1 - x] * other
                return carry

            lax.fori_loop(0, HALF, one, 0)

    def wait_halo(step, copies):
        for n in (2, 3, 4, 5, 0, 1):
            copies[n].wait_recv()
        for x in range(CX):
            base = x * HALF
            last = zs[step, base + HALF - 1].astype(f32)
            first = zs[step, base].astype(f32)
            got = halo_y[step, x, 0].astype(f32)
            edge[x, 0] = pltpu.roll(jnp.where(low64, last, got), COLS, 1)
            got = halo_y[step, x, 1].astype(f32)
            edge[x, 1] = pltpu.roll(jnp.where(low64, got, first), COLS, 1)

    def image(step, x, yy, prev, following):
        p = x * HALF + yy
        value = acc[p] - coef[p, x] * halo_x[step, x, yy].astype(f32)
        return value - coef[p, 2] * prev - coef[p, 3] * following

    def sweep(step, tail, count):
        def run(x, yy, prev, following, sums):
            p = x * HALF + yy
            terms = tail(p, image(step, x, yy, prev, following))
            return tuple(
                s + jnp.sum((a * b).reshape(8, 8, LANES), axis=0) for s, (a, b) in zip(sums, terms)
            )

        sums = (jnp.zeros((8, LANES), f32),) * count
        for x in range(CX):
            base = x * HALF

            def one(yy, sums):
                prev = zs[step, base + yy - 1].astype(f32)
                following = zs[step, base + yy + 1].astype(f32)
                return run(x, yy, prev, following, sums)

            sums = run(x, 0, edge[x, 0], zs[step, base + 1].astype(f32), sums)
            sums = lax.fori_loop(1, HALF - 1, one, sums)
            sums = run(x, HALF - 1, zs[step, base + HALF - 2].astype(f32), edge[x, 1], sums)
        rows = [jnp.sum(s, axis=0, keepdims=True) for s in sums]
        rows += [jnp.zeros((1, LANES), f32)] * (8 - count)
        return jnp.concatenate(rows, axis=0)

    def sum_start(step, payload):
        sum_send[step] = payload
        sum_group[step, group] = payload

        def push(d, carry):
            pltpu.make_async_remote_copy(
                src_ref=sum_send.at[step],
                dst_ref=sum_group.at[step, group],
                send_sem=g_ssem.at[step],
                recv_sem=g_rsem.at[step],
                device_id={"group": lax.rem(group + d, ng)},
                device_id_type=pl.DeviceIdType.MESH,
            ).start()
            return carry

        lax.fori_loop(1, ng, push, 0)

    def sum_middle(step):
        all_but_one(sum_group.at[step], ng, g_rsem.at[step]).wait()
        partial = jnp.sum(sum_group[step], axis=0)
        tot_send[step] = partial
        sum_bulk[step, bulk] = partial

        def push(d, carry):
            pltpu.make_async_remote_copy(
                src_ref=tot_send.at[step],
                dst_ref=sum_bulk.at[step, bulk],
                send_sem=b_ssem.at[step],
                recv_sem=b_rsem.at[step],
                device_id={"bulk": lax.rem(bulk + d, nb)},
                device_id_type=pl.DeviceIdType.MESH,
            ).start()
            return carry

        lax.fori_loop(1, nb, push, 0)

    def sum_finish(step, count):
        all_but_one(sum_bulk.at[step], nb, b_rsem.at[step]).wait()
        total = jnp.sum(sum_bulk[step], axis=0)
        total = total + pltpu.roll(total, COLS, 1)
        return [jnp.broadcast_to(total[i : i + 1], (8, LANES)) for i in range(count)]

    def scaled(factor, value):
        return (factor * value.reshape(8, 8, LANES)).reshape(NS, LANES)

    pl.semaphore_wait(barrier, ng + nb - 2)
    coarse_send(0, k0)

    for copy in prec_loads:
        copy.wait()
    local_part(k0)

    for copy in inv_loads:
        copy.wait()
    turned = [jnp.transpose(inv_raw[kh].reshape(ng * 16, AGGS * COMPS)) for kh in range(2)]
    high, low = split_hi_lo(jnp.concatenate(turned, axis=0))
    inv_rows[0 : 2 * AGGS * COMPS] = high
    inv_rows[2 * AGGS * COMPS :] = low

    for copy in diag_loads:
        copy.wait()

    def turn_diag(p, carry):
        both = diag_raw[p].astype(f32)
        diag_t[p, 0:NS] = jnp.transpose(both[:NS]).astype(bf16)
        diag_t[p, NS : 2 * NS] = jnp.transpose(both[NS:]).astype(bf16)
        return carry

    lax.fori_loop(0, PAIRS, turn_diag, 0)

    copies0 = finish_z(0)

    face_of = lax.broadcasted_iota(jnp.int32, (CY, 4 * NS), 1) // NS
    cell_y = lax.broadcasted_iota(jnp.int32, (CY, 4 * NS), 0)
    for x in range(CX):
        opened = face_ref[x].astype(f32)
        mask = jnp.zeros((CY, 4 * NS), f32)
        for f in range(4):
            mask = jnp.where(face_of == f, opened[:, f : f + 1], mask)
        if x == 0:
            mask = jnp.where((face_of == 0) & (bulk == 0), 0.0, mask)
        if x == CX - 1:
            mask = jnp.where((face_of == 1) & (bulk == nb - 1), 0.0, mask)
        mask = jnp.where((face_of == 2) & (cell_y == 0) & (group == 0), 0.0, mask)
        mask = jnp.where((face_of == 3) & (cell_y == CY - 1) & (group == ng - 1), 0.0, mask)
        value = coup_ref[x] * mask
        first = value.astype(bf16).astype(f32)
        second = (value - first).astype(bf16).astype(f32)
        third = value - first - second
        spread_rows = jnp.transpose(jnp.concatenate([first, second, third], axis=0)).astype(bf16)

        def expand(yy, carry):
            row = lax.broadcasted_iota(jnp.int32, (3 * CY, LANES), 0) & (CY - 1)
            lane = lax.broadcasted_iota(jnp.int32, (3 * CY, LANES), 1)
            pick = jnp.where(row == yy + jnp.where(lane < COLS, 0, HALF), 1.0, 0.0).astype(bf16)
            wide = mm(spread_rows, pick)
            for f in range(4):
                coef[x * HALF + yy, f] = wide[f * NS : (f + 1) * NS]
            return carry

        lax.fori_loop(0, HALF, expand, 0)

    own_image(0)
    wait_halo(0, copies0)

    def tail0(p, value):
        w0[p] = value
        start = k0[p]
        return ((start, start), (start, value), (value, value))

    payload = sweep(0, tail0, 3)

    coarse_send(1, w0)
    sum_start(0, payload)
    local_part(w0)
    sum_middle(0)
    copies1 = finish_z(1)
    own_image(1)
    wait_halo(1, copies1)
    sum_kk, sum_kw, sum_ww = sum_finish(0, 3)
    beta = jnp.sqrt(sum_kk + tiny_eps)
    s0 = 1.0 / beta
    h00 = sum_kw * s0 * s0
    g00 = sum_kk * s0 * s0
    left_sq = sum_ww * s0 * s0 - h00 * h00 * (2.0 - g00)
    h10u = jnp.sqrt(jnp.maximum(left_sq, 0.0) + tiny_eps)
    c1 = s0 / h10u
    c2 = h00 * s0 / h10u

    def tail1(p, value):
        image0 = w0[p]
        start = k0[p]
        vec = scaled(c1, image0) - scaled(c2, start)
        value = scaled(c1, value) - scaled(c2, image0)
        k1[p] = vec
        w1[p] = value
        return ((start, value), (vec, value), (value, value), (start, vec), (vec, vec))

    payload = sweep(1, tail1, 5)

    coarse_send(2, w1)
    sum_start(1, payload)
    local_part(w1)
    sum_middle(1)
    copies2 = finish_z(2)
    own_image(2)
    wait_halo(2, copies2)
    d_0w, d_1w, d_ww, d_01, d_11 = sum_finish(1, 5)
    h10 = jnp.sqrt(h10u * h10u * d_11 + tiny_eps)
    t1 = h10u / h10
    h01 = d_0w * s0 * t1
    h11 = d_1w * t1 * t1
    g01 = d_01 * s0 * t1
    g11 = d_11 * t1 * t1
    left_sq = (
        d_ww * t1 * t1
        - h01 * h01 * (2.0 - g00)
        - h11 * h11 * (2.0 - g11)
        + 2.0 * h01 * h11 * g01
    )
    h21u = jnp.sqrt(jnp.maximum(left_sq, 0.0) + tiny_eps)
    e1 = t1 / h21u
    e2 = h01 * s0 / h21u
    e3 = h11 * t1 / h21u

    def tail2(p, value):
        start = k0[p]
        vec1 = k1[p]
        image1 = w1[p]
        vec2 = scaled(e1, image1) - scaled(e2, start) - scaled(e3, vec1)
        value = scaled(e1, value) - scaled(e2, w0[p]) - scaled(e3, image1)
        return (
            (start, value),
            (vec1, value),
            (vec2, value),
            (value, value),
            (start, vec2),
            (vec1, vec2),
            (vec2, vec2),
        )

    payload = sweep(2, tail2, 7)
    sum_start(2, payload)
    sum_middle(2)
    q_0w, q_1w, q_2w, q_ww, q_02, q_12, q_22 = sum_finish(2, 7)
    h21 = jnp.sqrt(h21u * h21u * q_22 + tiny_eps)
    t2 = h21u / h21
    h02 = q_0w * s0 * t2
    h12 = q_1w * t1 * t2
    h22 = q_2w * t2 * t2
    g02 = q_02 * s0 * t2
    g12 = q_12 * t1 * t2
    g22 = q_22 * t2 * t2
    left_sq = (
        q_ww * t2 * t2
        - h02 * h02 * (2.0 - g00)
        - h12 * h12 * (2.0 - g11)
        - h22 * h22 * (2.0 - g22)
        + 2.0 * (h02 * h12 * g01 + h02 * h22 * g02 + h12 * h22 * g12)
    )
    h32 = jnp.sqrt(jnp.maximum(left_sq, 0.0) + tiny_eps)
    y0, y1, y2 = givens_solve([[h00, h10], [h01, h11, h21], [h02, h12, h22, h32]], beta)

    over = y2 * t2 / h21u
    a2 = over * t1
    on1 = y1 - over * h11
    a1 = on1 * t1 * c1
    a0 = y0 * s0 - over * h01 * s0 - on1 * t1 * c2

    def finish(p, carry):
        x = p // HALF
        yy = p % HALF
        total = (
            scaled(a0, zs[0, p].astype(f32))
            + scaled(a1, zs[1, p].astype(f32))
            + scaled(a2, zs[2, p].astype(f32))
        )
        out_ref[x, yy] = total[:, :COLS].astype(bf16)
        out_ref[x, yy + HALF] = pltpu.roll(total, COLS, 1)[:, :COLS].astype(bf16)
        return carry

    lax.fori_loop(0, PAIRS, finish, 0)

    for step, copies in enumerate((copies0, copies1, copies2)):
        all_but_one(res_buf.at[step], ng, res_ssem.at[step]).wait()
        all_but_one(sum_group.at[step], ng, g_ssem.at[step]).wait()
        all_but_one(sum_bulk.at[step], nb, b_ssem.at[step]).wait()
        for copy in copies:
            copy.wait_send()


def body(nb, ng, rhs, diag_blocks, precond_blocks, coupling, face_open, agg_id, coarse_basis, coarse_inv):
    rows = AGGS * COMPS
    inverse = coarse_inv.reshape(ng, 2, rows // 2, rows)
    any_spec = pl.BlockSpec(memory_space=pl.ANY)
    vmem_spec = pl.BlockSpec(memory_space=pltpu.VMEM)
    smem_spec = pl.BlockSpec(memory_space=pltpu.SMEM)
    field = pltpu.VMEM((PAIRS, NS, LANES), f32)
    dma = pltpu.SemaphoreType.DMA
    return pl.pallas_call(
        functools.partial(kernel, nb, ng),
        out_shape=jax.ShapeDtypeStruct(rhs.shape, bf16),
        in_specs=[any_spec, any_spec, any_spec, vmem_spec, vmem_spec, smem_spec, vmem_spec, any_spec],
        out_specs=vmem_spec,
        scratch_shapes=[
            pltpu.VMEM((CX, CY, NS, COLS), bf16),
            pltpu.VMEM((PAIRS, 2 * NS, NS), bf16),
            pltpu.VMEM((PAIRS, 2 * NS, NS), bf16),
            pltpu.VMEM((PAIRS, 2 * NS, NS), bf16),
            pltpu.VMEM((2, ng, rows // 2, rows), f32),
            pltpu.VMEM((4 * rows, ng * rows // 2), bf16),
            pltpu.VMEM((PAIRS, 4, NS, LANES), f32),
            pltpu.VMEM((PAIRS, AGGS, 8, LANES), f32),
            pltpu.VMEM((2, 2 * COMPS, NS), bf16),
            pltpu.VMEM((NS, 3 * COMPS), bf16),
            field,
            field,
            field,
            field,
            field,
            field,
            pltpu.VMEM((ITERS, PAIRS, NS, LANES), bf16),
            pltpu.VMEM((AGGS, NS, LANES), f32),
            pltpu.VMEM((ITERS, rows // 2, LANES), bf16),
            pltpu.VMEM((ITERS, ng, rows // 2, LANES), bf16),
            pltpu.VMEM((ITERS, CX, HALF, NS, LANES), bf16),
            pltpu.VMEM((ITERS, CX, 2, NS, LANES), bf16),
            pltpu.VMEM((CX, 2, NS, LANES), f32),
            pltpu.VMEM((ITERS, 8, LANES), f32),
            pltpu.VMEM((ITERS, ng, 8, LANES), f32),
            pltpu.VMEM((ITERS, 8, LANES), f32),
            pltpu.VMEM((ITERS, nb, 8, LANES), f32),
            dma((11,)),
            dma((ITERS,)),
            dma((ITERS,)),
            dma((ITERS, CX)),
            dma((ITERS, CX)),
            dma((ITERS, CX, 2)),
            dma((ITERS, CX, 2)),
            dma((ITERS,)),
            dma((ITERS,)),
            dma((ITERS,)),
            dma((ITERS,)),
        ],
        compiler_params=pltpu.CompilerParams(
            collective_id=0, has_side_effects=True, vmem_limit_bytes=40 * 1024 * 1024
        ),
        cost_estimate=pl.CostEstimate(flops=200_000_000, bytes_accessed=3_000_000, transcendentals=0),
    )(
        rhs,
        diag_blocks,
        precond_blocks,
        coupling,
        face_open,
        agg_id,
        coarse_basis,
        inverse,
    )


def solution(mesh):
    in_specs = (
        P("bulk", "group", None, None),
        P("bulk", "group", None, None),
        P("bulk", "group", None, None),
        P("bulk", "group", None),
        P("bulk", "group", None),
        P("bulk", "group"),
        P(),
        P("bulk", None, "group"),
    )
    out_specs = P("bulk", "group", None, None)
    return jax.shard_map(
        functools.partial(body, mesh.shape["bulk"], mesh.shape["group"]),
        mesh=mesh,
        in_specs=in_specs,
        out_specs=out_specs,
        check_vma=False,
    )
```

time: 881 us -> 80.2 us (0.09)
  blocking collectives: 589 us -> 0 us
  waiting for transfers between devices: 193 us -> 0 us
  Pallas kernels: 0 us -> 73.3 us
  starting transfers between devices: 37.9 us -> 0 us
  matrix products: 20.1 us -> 0 us
  between operations: 13.6 us -> 0.04 us
  local copies, waits for them, and re-layouts: 16.8 us -> 6.43 us
  other arithmetic: 9.21 us -> 0 us
    psum x6 -> x0, blocking collectives: 589 us -> none  [the longest x3 284 us: body(): lax.psum(jnp.sum(image * image, axis=(0, 1, 2)), ('bulk', 'group'))]
    reduce_scatter x3 -> x0, waiting for transfers between devices: 167 us -> none  [body(): lax.psum_scatter(jnp.dot(inverse_cols, residual, precision=highest), 'gro...]
    pallas_call x0 -> x1, Pallas kernels: none -> 73.3 us  [body(): pl.pallas_call(functools.partial(kernel, nb, ng), out_shape=jax.ShapeDtyp...]
    ppermute x12 -> x0, starting transfers between devices: 37.8 us -> none  [the longest x6 25.5 us: padded_2(): lax.ppermute(tail, axis, [(i, (i + 1) % count) for i in range(ends)])]
    ppermute x12 -> x0, waiting for transfers between devices: 25.5 us -> none  [the longest x6 19.7 us: padded_2(): lax.ppermute(head, axis, [((i + 1) % count, i) for i in range(ends)])]
    dot_general x21 -> x0, matrix products: 20.1 us -> none  [the longest x3 6.93 us: body(): jnp.einsum('xyij,xyir->xyjr', diag_blocks, zvec, preferred_element_type=j...]
  transfers between devices with their start and end apart: 15 -> 0, of which waited for: 12 -> 0; matrix products, arithmetic and copies ran while one was open for 0% -> 0% of each run, Pallas kernels for 0% -> 0%
where the time goes in v1:
time: 80.2 us; the launch traced here: 79.8 us
  Pallas kernels  73.3 us (91%)
  local copies, waits for them, and re-layouts  6.43 us (8%)
    pallas_call x1, Pallas kernels, body(): pl.pallas_call(functools.partial(kernel, nb, ng), out_shape=jax.ShapeDtyp...  73.3 us
    unnamed x16, local copies, waits for them, and re-layouts  6.43 us

profile of v1, /device:TPU:1, one launch (start us, length us, event | category | flops | bytes accessed | tf_op | source)
XLA Modules:
  0.0 79.8 jit_solution(15174190281695676986)
XLA Ops:
  0.0 0.0 copy-start.5
  0.0 0.8 copy.10.face_ref
  0.8 0.0 copy-done.5
  0.8 0.1 copy.11.basis_ref
  0.9 0.0 copy-start.3
  0.9 1.0 %copy.9 = f32[1,512,32]{2,1,0:T(8,128)S(1)} copy(f32[1,512,32]{1,2,0:T(8,128)} %param.15) | data formatting | bytes 131072 | tf_op args[7]
  1.8 0.0 copy-start.4
  1.9 0.0 copy-done.3
  1.9 0.7 copy-done.4
  2.5 0.0 copy-start
  2.5 1.0 %copy-done = bf16[2,16,64,64]{3,2,1,0:T(8,128)(2,1)S(1)} copy-done((bf16[2,16,64,64]{3,2,1,0:T(8,128)(2,1)S(1)}, bf16[2,16,64,64]{3,2,1,0:T(8,128)(2,1)}, u32[]{:S(2)}) %copy-start) | copy-done | bytes 262168
  3.6 0.0 copy-start.1
  3.6 1.0 %copy-done.1 = bf16[2,16,64,64]{3,2,1,0:T(8,128)(2,1)S(1)} copy-done((bf16[2,16,64,64]{3,2,1,0:T(8,128)(2,1)S(1)}, bf16[2,16,64,64]{3,2,1,0:T(8,128)(2,1)}, u32[]{:S(2)}) %copy-start.1) | copy-done | bytes 262168
  4.6 0.0 copy-start.2
  4.6 1.0 %copy-done.2 = bf16[2,16,64,64]{3,2,1,0:T(8,128)(2,1)S(1)} copy-done((bf16[2,16,64,64]{3,2,1,0:T(8,128)(2,1)S(1)}, bf16[2,16,64,64]{3,2,1,0:T(8,128)(2,1)}, u32[]{:S(2)}) %copy-start.2) | copy-done | bytes 262168
  5.7 73.3 %shard_map.82 = bf16[2,16,64,64]{3,2,1,0:T(8,128)(2,1)S(1)} custom-call(bf16[2,16,64,64]{3,2,1,0:T(8,128)(2,1)S(1)} %copy-done, bf16[2,16,64,64]{3,2,1,0:T(8,128)(2,1)S(1)} %copy-done.1, bf16[2,16,64,64]{3,2,1,0:T(8,128)(2,1)S(1)} %copy-done.2, f32[2,16,256]{2,1,0:T(8,128)S(1)} %copy-done.3, s32[2,16,4]{2,1,0:T(8,128)S(1)} %copy.10.face_ref, ...), custom_call_target="tpu_custom_call" | custom-call | flops 200000000 | bytes 3000000 | tf_op jit(solution)/shard_map/pallas_call | solution.py:612
  79.0 0.8 copy.13
Async XLA Ops:
  0.0 0.8 copy-start.5
  0.9 1.0 %copy-start.3 = (f32[2,16,256]{2,1,0:T(8,128)S(1)}, f32[2,16,256]{2,1,0:T(8,128)}, u32[]{:S(2)}) copy-start(f32[2,16,256]{2,1,0:T(8,128)} %coup_ref.1) | copy-start | bytes 98308
  1.8 0.7 copy-start.4
  2.5 1.0 %copy-start = (bf16[2,16,64,64]{3,2,1,0:T(8,128)(2,1)S(1)}, bf16[2,16,64,64]{3,2,1,0:T(8,128)(2,1)}, u32[]{:S(2)}) copy-start(bf16[2,16,64,64]{3,2,1,0:T(8,128)(2,1)} %rhs_hbm.1) | copy-start | bytes 786436
  3.6 1.0 %copy-start.1 = (bf16[2,16,64,64]{3,2,1,0:T(8,128)(2,1)S(1)}, bf16[2,16,64,64]{3,2,1,0:T(8,128)(2,1)}, u32[]{:S(2)}) copy-start(bf16[2,16,64,64]{3,2,1,0:T(8,128)(2,1)} %diag_hbm.1) | copy-start | bytes 786436
  4.6 1.0 %copy-start.2 = (bf16[2,16,64,64]{3,2,1,0:T(8,128)(2,1)S(1)}, bf16[2,16,64,64]{3,2,1,0:T(8,128)(2,1)}, u32[]{:S(2)}) copy-start(bf16[2,16,64,64]{3,2,1,0:T(8,128)(2,1)} %prec_hbm.1) | copy-start | bytes 786436

commit v2 on v1

--- a/solution.py
+++ b/solution.py
@@ -17,6 +17,7 @@
 HALF = CY // 2
 PAIRS = CX * HALF
 LANES = 2 * COLS
+UNROLL = 16
 
 tiny_eps = 1e-06
 f32 = jnp.float32
@@ -31,6 +32,19 @@
 
 def mm(left, right):
     return jnp.dot(left, right, preferred_element_type=f32)
+
+
+def loop(count, step, carry=0, unroll=UNROLL):
+    unroll = min(unroll, count)
+
+    def several(start, carry):
+        for i in range(unroll):
+            carry = step(start * unroll + i, carry)
+        return carry
+
+    if unroll == count:
+        return several(0, carry)
+    return lax.fori_loop(0, count // unroll, several, carry)
 
 
 def low_half(shape):
@@ -76,12 +90,15 @@
     rhs_hbm,
     diag_hbm,
     prec_hbm,
+    coup_hbm,
+    face_hbm,
+    agg_ref,
+    basis_hbm,
+    inv_hbm,
+    out_ref,
     coup_ref,
     face_ref,
-    agg_ref,
     basis_ref,
-    inv_hbm,
-    out_ref,
     rhs_raw,
     prec,
     diag_raw,
@@ -138,11 +155,13 @@
             diag_loads.append(
                 pltpu.make_async_copy(diag_hbm.at[src], diag_raw.at[dst], load_sem.at[5 + n])
             )
-    inv_loads = [
-        pltpu.make_async_copy(inv_hbm.at[:, kh], inv_raw.at[kh], load_sem.at[9 + kh])
-        for kh in range(2)
+    inv_loads = [pltpu.make_async_copy(inv_hbm, inv_raw, load_sem.at[9])]
+    small_loads = [
+        pltpu.make_async_copy(basis_hbm, basis_ref, load_sem.at[10]),
+        pltpu.make_async_copy(face_hbm, face_ref, load_sem.at[11]),
+        pltpu.make_async_copy(coup_hbm, coup_ref, load_sem.at[12]),
     ]
-    for copy in loads + prec_loads + inv_loads + diag_loads:
+    for copy in loads + small_loads + prec_loads + inv_loads + diag_loads:
         copy.start()
 
     barrier = pltpu.get_barrier_semaphore()
@@ -184,11 +203,11 @@
             )
         return carry
 
-    lax.fori_loop(0, PAIRS, make_weights, 0)
+    loop(PAIRS, make_weights)
 
     weight_scale = (AGGS / (CX * CY)) ** 0.5
-    basis = basis_ref[...]
-    turned = jnp.transpose(basis)
+    small_loads[0].wait()
+    turned = basis_ref[...]
     high, low = split_hi_lo(turned)
     stacked = jnp.concatenate([high.astype(f32), high.astype(f32), low.astype(f32)], axis=0)
     bas_w[...] = jnp.transpose(stacked).astype(bf16)
@@ -206,7 +225,7 @@
         k0[p] = jnp.concatenate([first, second], axis=1)
         return carry
 
-    lax.fori_loop(0, PAIRS, make_start, 0)
+    loop(PAIRS, make_start)
 
     def coarse_send(step, field):
         def add(p, sums):
@@ -214,7 +233,7 @@
             return tuple(sums[k] + wtab[p, k] * value for k in range(AGGS))
 
         zero = jnp.zeros((8, 8, LANES), f32)
-        sums = lax.fori_loop(0, PAIRS, add, (zero,) * AGGS)
+        sums = loop(PAIRS, add, (zero,) * AGGS)
         sums = [s.reshape(NS, LANES) for s in sums]
         parts = []
         for kl in range(2):
@@ -253,7 +272,7 @@
             local_y[p] = pair_product(prec, p, field[p].astype(bf16))
             return carry
 
-        lax.fori_loop(0, PAIRS, one, 0)
+        loop(PAIRS, one)
 
     def halo_copies(step):
         left = lax.rem(bulk + nb - 1, nb)
@@ -288,9 +307,10 @@
 
     def finish_z(step):
         all_but_one(res_buf.at[step], ng, res_rsem.at[step]).wait()
-        gathered = res_buf[step].reshape(ng * 16, LANES)
+        rows = AGGS * COMPS
+        gathered = res_buf[step]
+        gathered = jnp.concatenate([gathered, gathered], axis=1).reshape(ng * rows, LANES)
         both = mm(inv_rows[...], gathered)
-        rows = AGGS * COMPS
         both = both[: 2 * rows] + both[2 * rows :]
         mixed = jnp.where(low_half((rows, LANES)), both[:rows], both[rows:])
         cor = mixed + pltpu.roll(mixed, COLS, 1)
@@ -302,16 +322,15 @@
             spread[k] = wide[:, k * LANES : (k + 1) * LANES]
         copies = halo_copies(step)
 
-        def one(p, carry):
-            x = p // HALF
-            yy = p % HALF
+        def one(x, yy, carry):
+            p = x * HALF + yy
             first = spread[agg_ref[x, yy]]
             second = spread[agg_ref[x, yy + HALF]]
             zs[step, p] = (local_y[p] + jnp.where(low64, first, second)).astype(bf16)
             return carry
 
         for x in range(CX):
-            lax.fori_loop(x * HALF, (x + 1) * HALF, one, 0)
+            loop(HALF, functools.partial(one, x))
             copies[x].start()
             copies[2 + 2 * x].start()
             copies[3 + 2 * x].start()
@@ -327,7 +346,7 @@
                 acc[p] = own - coef[p, 1 - x] * other
                 return carry
 
-            lax.fori_loop(0, HALF, one, 0)
+            loop(HALF, one)
 
     def wait_halo(step, copies):
         for n in (2, 3, 4, 5, 0, 1):
@@ -358,13 +377,14 @@
         for x in range(CX):
             base = x * HALF
 
-            def one(yy, sums):
+            def one(row, sums):
+                yy = row + 1
                 prev = zs[step, base + yy - 1].astype(f32)
                 following = zs[step, base + yy + 1].astype(f32)
                 return run(x, yy, prev, following, sums)
 
             sums = run(x, 0, edge[x, 0], zs[step, base + 1].astype(f32), sums)
-            sums = lax.fori_loop(1, HALF - 1, one, sums)
+            sums = loop(HALF - 2, one, sums)
             sums = run(x, HALF - 1, zs[step, base + HALF - 2].astype(f32), edge[x, 1], sums)
         rows = [jnp.sum(s, axis=0, keepdims=True) for s in sums]
         rows += [jnp.zeros((1, LANES), f32)] * (8 - count)
@@ -424,10 +444,15 @@
 
     for copy in inv_loads:
         copy.wait()
-    turned = [jnp.transpose(inv_raw[kh].reshape(ng * 16, AGGS * COMPS)) for kh in range(2)]
-    high, low = split_hi_lo(jnp.concatenate(turned, axis=0))
-    inv_rows[0 : 2 * AGGS * COMPS] = high
-    inv_rows[2 * AGGS * COMPS :] = low
+    rows = AGGS * COMPS
+    turned = inv_raw[...]
+    in_half = (lax.broadcasted_iota(jnp.int32, turned.shape, 1) & (rows - 1)) < rows // 2
+    turned = jnp.concatenate(
+        [jnp.where(in_half, turned, 0.0), jnp.where(in_half, 0.0, turned)], axis=0
+    )
+    high, low = split_hi_lo(turned)
+    inv_rows[0 : 2 * rows] = high
+    inv_rows[2 * rows :] = low
 
     for copy in diag_loads:
         copy.wait()
@@ -438,14 +463,16 @@
         diag_t[p, NS : 2 * NS] = jnp.transpose(both[NS:]).astype(bf16)
         return carry
 
-    lax.fori_loop(0, PAIRS, turn_diag, 0)
+    loop(PAIRS, turn_diag)
 
     copies0 = finish_z(0)
 
+    small_loads[1].wait()
+    small_loads[2].wait()
     face_of = lax.broadcasted_iota(jnp.int32, (CY, 4 * NS), 1) // NS
     cell_y = lax.broadcasted_iota(jnp.int32, (CY, 4 * NS), 0)
     for x in range(CX):
-        opened = face_ref[x].astype(f32)
+        opened = jnp.transpose(face_ref[x].astype(f32))
         mask = jnp.zeros((CY, 4 * NS), f32)
         for f in range(4):
             mask = jnp.where(face_of == f, opened[:, f : f + 1], mask)
@@ -470,7 +497,7 @@
                 coef[x * HALF + yy, f] = wide[f * NS : (f + 1) * NS]
             return carry
 
-        lax.fori_loop(0, HALF, expand, 0)
+        loop(HALF, expand)
 
     own_image(0)
     wait_halo(0, copies0)
@@ -591,7 +618,7 @@
         out_ref[x, yy + HALF] = pltpu.roll(total, COLS, 1)[:, :COLS].astype(bf16)
         return carry
 
-    lax.fori_loop(0, PAIRS, finish, 0)
+    loop(PAIRS, finish)
 
     for step, copies in enumerate((copies0, copies1, copies2)):
         all_but_one(res_buf.at[step], ng, res_ssem.at[step]).wait()
@@ -603,7 +630,7 @@
 
 def body(nb, ng, rhs, diag_blocks, precond_blocks, coupling, face_open, agg_id, coarse_basis, coarse_inv):
     rows = AGGS * COMPS
-    inverse = coarse_inv.reshape(ng, 2, rows // 2, rows)
+    inverse = jnp.swapaxes(coarse_inv[0], 0, 1)
     any_spec = pl.BlockSpec(memory_space=pl.ANY)
     vmem_spec = pl.BlockSpec(memory_space=pltpu.VMEM)
     smem_spec = pl.BlockSpec(memory_space=pltpu.SMEM)
@@ -612,15 +639,18 @@
     return pl.pallas_call(
         functools.partial(kernel, nb, ng),
         out_shape=jax.ShapeDtypeStruct(rhs.shape, bf16),
-        in_specs=[any_spec, any_spec, any_spec, vmem_spec, vmem_spec, smem_spec, vmem_spec, any_spec],
+        in_specs=[any_spec, any_spec, any_spec, any_spec, any_spec, smem_spec, any_spec, any_spec],
         out_specs=vmem_spec,
         scratch_shapes=[
+            pltpu.VMEM((CX, CY, 4 * NS), f32),
+            pltpu.VMEM((CX, 4, CY), jnp.int32),
+            pltpu.VMEM((COMPS, NS), f32),
             pltpu.VMEM((CX, CY, NS, COLS), bf16),
             pltpu.VMEM((PAIRS, 2 * NS, NS), bf16),
             pltpu.VMEM((PAIRS, 2 * NS, NS), bf16),
             pltpu.VMEM((PAIRS, 2 * NS, NS), bf16),
-            pltpu.VMEM((2, ng, rows // 2, rows), f32),
-            pltpu.VMEM((4 * rows, ng * rows // 2), bf16),
+            pltpu.VMEM((rows, ng * rows), f32),
+            pltpu.VMEM((4 * rows, ng * rows), bf16),
             pltpu.VMEM((PAIRS, 4, NS, LANES), f32),
             pltpu.VMEM((PAIRS, AGGS, 8, LANES), f32),
             pltpu.VMEM((2, 2 * COMPS, NS), bf16),
@@ -642,7 +672,7 @@
             pltpu.VMEM((ITERS, ng, 8, LANES), f32),
             pltpu.VMEM((ITERS, 8, LANES), f32),
             pltpu.VMEM((ITERS, nb, 8, LANES), f32),
-            dma((11,)),
+            dma((13,)),
             dma((ITERS,)),
             dma((ITERS,)),
             dma((ITERS, CX)),
@@ -655,7 +685,7 @@
             dma((ITERS,)),
         ],
         compiler_params=pltpu.CompilerParams(
-            collective_id=0, has_side_effects=True, vmem_limit_bytes=40 * 1024 * 1024
+            collective_id=0, has_side_effects=True, vmem_limit_bytes=60 * 1024 * 1024
         ),
         cost_estimate=pl.CostEstimate(flops=200_000_000, bytes_accessed=3_000_000, transcendentals=0),
     )(
@@ -663,9 +693,9 @@
         diag_blocks,
         precond_blocks,
         coupling,
-        face_open,
+        jnp.swapaxes(face_open, 1, 2),
         agg_id,
-        coarse_basis,
+        jnp.swapaxes(coarse_basis, 0, 1),
         inverse,
     )
 

time: 80.2 us -> 74.1 us (0.924)
  local copies, waits for them, and re-layouts: 6.43 us -> 1.87 us
  Pallas kernels: 73.3 us -> 72.1 us
    unnamed x16 -> x1, local copies, waits for them, and re-layouts: 6.43 us -> 1.87 us
    pallas_call x1, Pallas kernels: 73.3 us -> 72.1 us  [body(): pl.pallas_call(functools.partial(kernel, nb, ng), out_shape=jax.ShapeDtyp...]
where the time goes in v2:
time: 74.1 us; the launch traced here: 73.9 us
  Pallas kernels  72.1 us (97%)
  local copies, waits for them, and re-layouts  1.87 us (3%)
    pallas_call x1, Pallas kernels, body(): pl.pallas_call(functools.partial(kernel, nb, ng), out_shape=jax.ShapeDtyp...  72.1 us
    unnamed x1, local copies, waits for them, and re-layouts  1.87 us

profile of v2, /device:TPU:1, one launch (start us, length us, event | category | flops | bytes accessed | tf_op | source)
XLA Modules:
  0.0 73.9 jit_solution(10007062037910566456)
XLA Ops:
  0.0 72.1 %shard_map.82 = bf16[2,16,64,64]{3,2,1,0:T(8,128)(2,1)} custom-call(bf16[2,16,64,64]{3,2,1,0:T(8,128)(2,1)} %rhs_hbm.1, bf16[2,16,64,64]{3,2,1,0:T(8,128)(2,1)} %diag_hbm.1, bf16[2,16,64,64]{3,2,1,0:T(8,128)(2,1)} %prec_hbm.1, f32[2,16,256]{2,1,0:T(8,128)} %coup_hbm.1, s32[2,4,16]{2,1,0:T(4,128)} %bitcast.6, s32[2,16]{1,0:T(2,128)} %agg_ref.1, ...), custom_call_target="tpu_custom_call" | custom-call | flops 200000000 | bytes 3000000 | tf_op jit(solution)/shard_map/pallas_call | solution.py:639
  72.1 1.9 %copy.10 = bf16[2,16,64,64]{3,2,1,0:T(8,128)(2,1)} copy(bf16[2,16,64,64]{3,2,1,0:T(8,128)(2,1)} %shard_map.82) | data formatting | bytes 524288

commit v3 on v2

v3 whole, which is shorter than its diff:
```python
import functools

import jax
import jax.numpy as jnp
from jax import lax
from jax.experimental import pallas as pl
from jax.experimental.pallas import tpu as pltpu
from jax.sharding import PartitionSpec as P

NS = 64
COLS = 64
CX = 2
CY = 16
AGGS = 4
COMPS = 8
ITERS = 3
HALF = CY // 2
PAIRS = CX * HALF
LANES = 2 * COLS
UNROLL = 16

tiny_eps = 1e-06
f32 = jnp.float32
bf16 = jnp.bfloat16


def split_hi_lo(value):
    high = value.astype(bf16)
    low = (value - high.astype(f32)).astype(bf16)
    return high, low


def mm(left, right):
    return jnp.dot(left, right, preferred_element_type=f32)


def loop(count, step, carry=0, unroll=UNROLL):
    unroll = min(unroll, count)

    def several(start, carry):
        for i in range(unroll):
            carry = step(start * unroll + i, carry)
        return carry

    if unroll == count:
        return several(0, carry)
    return lax.fori_loop(0, count // unroll, several, carry)


def far_first(count):
    return sorted(range(1, count), key=lambda d: -min(d, count - d))


def far_targets(nb, bulk):
    along = 8 if nb % 8 == 0 else nb
    across = nb // along

    def hops(d):
        high, low = d // along, d % along
        return min(high, across - high) + min(low, along - low)

    base = (bulk // along) * along
    return [
        {"bulk": lax.rem(base + (d // along) * along, nb) + lax.rem(bulk + d % along, along)}
        for d in sorted(range(1, nb), key=lambda d: -hops(d))
    ]


def low_half(shape):
    return lax.broadcasted_iota(jnp.int32, shape, 1) < COLS


def givens_solve(hessen_cols, beta_norm):
    cosine_list = []
    sine_list = []
    target = [beta_norm] + [jnp.zeros_like(beta_norm) for _ in range(ITERS)]
    triangle = []
    for section in range(ITERS):
        column = list(hessen_cols[section])
        for earlier in range(section):
            upper = column[earlier]
            lower = column[earlier + 1]
            column[earlier] = cosine_list[earlier] * upper + sine_list[earlier] * lower
            column[earlier + 1] = -sine_list[earlier] * upper + cosine_list[earlier] * lower
        upper = column[section]
        lower = column[section + 1]
        radius = jnp.sqrt(upper * upper + lower * lower)
        cosine = upper / radius
        sine_val = lower / radius
        cosine_list.append(cosine)
        sine_list.append(sine_val)
        column[section] = radius
        carried = target[section]
        target[section] = cosine * carried
        target[section + 1] = -sine_val * carried
        triangle.append(column[: section + 1])
    result = [None] * ITERS
    for section in reversed(range(ITERS)):
        accumulated = target[section]
        for later in range(section + 1, ITERS):
            accumulated = accumulated - triangle[later][section] * result[later]
        result[section] = accumulated / triangle[section][section]
    return result


def kernel(
    nb,
    ng,
    rhs_hbm,
    diag_hbm,
    prec_hbm,
    coup_hbm,
    face_hbm,
    agg_ref,
    basis_hbm,
    inv_hbm,
    out_ref,
    coup_ref,
    face_ref,
    basis_ref,
    rhs_raw,
    prec,
    diag_raw,
    diag_t,
    inv_raw,
    inv_rows,
    coef,
    wtab,
    bas_t,
    bas_w,
    k0,
    w0,
    w1,
    acc,
    yb,
    zs,
    spread,
    res_send,
    res_buf,
    cor_send,
    cor_buf,
    halo_x,
    halo_y,
    wnb_x,
    wnb_y,
    sum_send,
    sum_group,
    tot_send,
    sum_bulk,
    load_sem,
    res_ssem,
    res_rsem,
    cor_ssem,
    cor_rsem,
    hx_ssem,
    hx_rsem,
    hy_ssem,
    hy_rsem,
    g_ssem,
    g_rsem,
    b_ssem,
    b_rsem,
):
    bulk = lax.axis_index("bulk")
    group = lax.axis_index("group")

    loads = [pltpu.make_async_copy(rhs_hbm, rhs_raw, load_sem.at[0])]
    prec_loads = []
    diag_loads = []
    for x in range(CX):
        for yh in range(2):
            n = x * 2 + yh
            src = (x, pl.ds(yh * HALF, HALF))
            dst = (pl.ds(x * HALF, HALF), pl.ds(yh * NS, NS))
            prec_loads.append(
                pltpu.make_async_copy(prec_hbm.at[src], prec.at[dst], load_sem.at[1 + n])
            )
            diag_loads.append(
                pltpu.make_async_copy(diag_hbm.at[src], diag_raw.at[dst], load_sem.at[5 + n])
            )
    inv_loads = [pltpu.make_async_copy(inv_hbm, inv_raw, load_sem.at[9])]
    small_loads = [
        pltpu.make_async_copy(basis_hbm, basis_ref, load_sem.at[10]),
        pltpu.make_async_copy(face_hbm, face_ref, load_sem.at[11]),
        pltpu.make_async_copy(coup_hbm, coup_ref, load_sem.at[12]),
    ]
    for copy in loads + small_loads + prec_loads + inv_loads + diag_loads:
        copy.start()

    barrier = pltpu.get_barrier_semaphore()

    near_group = [{"group": lax.rem(group + d, ng)} for d in far_first(ng)]
    far_bulk = far_targets(nb, bulk)
    for target in near_group + far_bulk:
        pl.semaphore_signal(barrier, inc=1, device_id=target, device_id_type=pl.DeviceIdType.MESH)

    rows = AGGS * COMPS
    low8 = low_half((8, LANES))
    low16 = low_half((rows // 2, LANES))
    low32 = low_half((rows, LANES))
    low64 = low_half((NS, LANES))
    row8 = lax.broadcasted_iota(jnp.int32, (8, LANES), 0)

    def make_weights(p, carry):
        x = p // HALF
        yy = p % HALF
        cell = jnp.where(low8, agg_ref[x, yy], agg_ref[x, yy + HALF])
        wtab[p] = jnp.where(cell == row8, 1.0, 0.0).astype(f32)
        return carry

    loop(PAIRS, make_weights)

    weight_scale = (AGGS / (CX * CY)) ** 0.5
    small_loads[0].wait()
    turned = basis_ref[...]
    high, low = split_hi_lo(turned)
    stacked = jnp.concatenate([high.astype(f32), high.astype(f32), low.astype(f32)], axis=0)
    bas_w[...] = jnp.transpose(stacked).astype(bf16)
    high, low = split_hi_lo(turned * weight_scale)
    bas_t[0] = jnp.concatenate([high, high], axis=0)
    bas_t[1] = jnp.concatenate([low, low], axis=0)

    loads[0].wait()

    def make_start(p, carry):
        x = p // HALF
        yy = p % HALF
        first = rhs_raw[x, yy].astype(f32)
        second = rhs_raw[x, yy + HALF].astype(f32)
        k0[p] = jnp.concatenate([first, second], axis=1)
        return carry

    loop(PAIRS, make_start)

    def remote(src, dst, ssem, rsem, target):
        return pltpu.make_async_remote_copy(
            src_ref=src,
            dst_ref=dst,
            send_sem=ssem,
            recv_sem=rsem,
            device_id=target,
            device_id_type=pl.DeviceIdType.MESH,
        )

    def all_but_one(buf, count, sem):
        return pltpu.make_async_copy(buf.at[pl.ds(0, count - 1)], buf.at[pl.ds(0, count - 1)], sem)

    def coarse_residual(step, field):
        def add(p, sums):
            value = field[p].reshape(8, 8, LANES)
            return tuple(sums[k] + wtab[p, k : k + 1] * value for k in range(AGGS))

        zero = jnp.zeros((8, 8, LANES), f32)
        sums = loop(PAIRS, add, (zero,) * AGGS)
        sums = [s.reshape(NS, LANES) for s in sums]
        parts = []
        for kl in range(2):
            keep = jnp.where(low64, sums[kl], sums[kl + 2])
            move = jnp.where(low64, sums[kl + 2], sums[kl])
            total = keep + pltpu.roll(move, COLS, 1)
            high, low = split_hi_lo(total)
            part = mm(bas_t[0], high) + mm(bas_t[0], low) + mm(bas_t[1], high)
            parts.append(part[:COMPS])
        res = jnp.concatenate(parts, axis=0).astype(bf16)
        res_send[step] = res
        res_buf[step, group] = res

    def coarse_push(step):
        for target in near_group:
            remote(
                res_send.at[step], res_buf.at[step, group], res_ssem.at[step], res_rsem.at[step], target
            ).start()

    def pair_product(mats, p, value):
        both = mm(mats[p], value)
        return jnp.where(low64, both[:NS], both[NS:])

    left = {"bulk": lax.rem(bulk + nb - 1, nb)}
    right = {"bulk": lax.rem(bulk + 1, nb)}
    before = {"group": lax.rem(group + ng - 1, ng)}
    after = {"group": lax.rem(group + 1, ng)}

    def edge_copies(src, dst_x, dst_y, n):
        copies = []
        for x, side in ((0, left), (1, right)):
            copies.append(
                remote(
                    src.at[pl.ds(x * HALF, HALF)],
                    dst_x.at[1 - x],
                    hx_ssem.at[n, x],
                    hx_rsem.at[n, 1 - x],
                    side,
                )
            )
        for x in range(CX):
            for end, row, side in ((0, HALF - 1, after), (1, 0, before)):
                copies.append(
                    remote(
                        src.at[x * HALF + row],
                        dst_y.at[x, end],
                        hy_ssem.at[n, x, end],
                        hy_rsem.at[n, x, end],
                        side,
                    )
                )
        return copies

    def local_part(step, field):
        copies = edge_copies(yb.at[step], halo_x.at[step], halo_y.at[step], step)

        def one(x, yy, carry):
            p = x * HALF + yy
            yb[step, p] = pair_product(prec, p, field[p].astype(bf16)).astype(bf16)
            return carry

        for x in range(CX):
            loop(HALF, functools.partial(one, x))
            copies[x].start()
            copies[2 + 2 * x].start()
            copies[3 + 2 * x].start()
        return copies

    def make_spread(n, cor):
        wide = jnp.concatenate([cor[k * COMPS : (k + 1) * COMPS] for k in range(AGGS)], axis=1)
        high, low = split_hi_lo(wide)
        wide = jnp.concatenate([high.astype(f32), low.astype(f32), high.astype(f32)], axis=0)
        wide = mm(bas_w[...], wide.astype(bf16))
        for k in range(AGGS):
            spread[n, k] = wide[:, k * LANES : (k + 1) * LANES]

    def cor_copies(step):
        return [
            remote(
                cor_send.at[step],
                cor_buf.at[step, slot],
                cor_ssem.at[step, slot],
                cor_rsem.at[step, slot],
                side,
            )
            for slot, side in ((0, right), (1, left), (2, after), (3, before))
        ]

    def coarse_solve(step):
        all_but_one(res_buf.at[step], ng, res_rsem.at[step]).wait()
        gathered = res_buf[step]
        gathered = jnp.concatenate([gathered, gathered], axis=1).reshape(ng * rows, LANES)
        both = mm(inv_rows[...], gathered)
        both = both[: 2 * rows] + both[2 * rows :]
        mixed = jnp.where(low32, both[:rows], both[rows:])
        cor = mixed + pltpu.roll(mixed, COLS, 1)
        cor_send[step] = jnp.where(low16, cor[: rows // 2], cor[rows // 2 :])
        copies = cor_copies(step)
        for copy in copies:
            copy.start()
        make_spread(4, cor)
        return copies

    def joined(n, weights, local):
        total = local.astype(f32).reshape(8, 8, LANES)
        for k in range(AGGS):
            total = total + weights[k : k + 1] * spread[n, k].reshape(8, 8, LANES)
        return total.reshape(NS, LANES).astype(bf16)

    def own_z(step):
        def one(p, carry):
            zs[step, p] = joined(4, wtab[p], yb[step, p])
            return carry

        loop(PAIRS, one)

    def own_image(step):
        def one(p, carry):
            x = p // HALF
            yy = p % HALF
            value = pair_product(diag_t, p, zs[step, p])
            value = value - coef[p, 1 - x] * zs[step, (1 - x) * HALF + yy].astype(f32)
            if yy > 0:
                value = value - coef[p, 2] * zs[step, p - 1].astype(f32)
            if yy < HALF - 1:
                value = value - coef[p, 3] * zs[step, p + 1].astype(f32)
            acc[p] = value
            return carry

        loop(PAIRS, one)

    def wait_edges(step, halos, cors):
        for n in range(4):
            cors[n].wait_recv()
        for n in range(4):
            got = cor_buf[step, n]
            swapped = pltpu.roll(got, COLS, 1)
            make_spread(
                n,
                jnp.concatenate(
                    [jnp.where(low16, got, swapped), jnp.where(low16, swapped, got)], axis=0
                ),
            )
        for copy in halos:
            copy.wait_recv()

    def sweep(step, tail, count):
        sums = [jnp.zeros((8, LANES), f32)] * count
        for p in range(PAIRS):
            x = p // HALF
            yy = p % HALF
            beside = joined(x, wnb_x[x, yy], halo_x[step, x, yy]).astype(f32)
            value = acc[p] - coef[p, x] * beside
            if yy == 0:
                got = joined(2, wnb_y[x, 0], halo_y[step, x, 0]).astype(f32)
                own = zs[step, p + HALF - 1].astype(f32)
                value = value - coef[p, 2] * pltpu.roll(jnp.where(low64, own, got), COLS, 1)
            if yy == HALF - 1:
                got = joined(3, wnb_y[x, 1], halo_y[step, x, 1]).astype(f32)
                own = zs[step, p - HALF + 1].astype(f32)
                value = value - coef[p, 3] * pltpu.roll(jnp.where(low64, got, own), COLS, 1)
            terms = tail(p, value)
            sums = [
                s + jnp.sum((a * b).reshape(8, 8, LANES), axis=0) for s, (a, b) in zip(sums, terms)
            ]
        if not sums:
            return None
        sums = [jnp.sum(s, axis=0, keepdims=True) for s in sums]
        sums += [sums[-1]] * (count % 2)
        first = jnp.concatenate(sums[0::2], axis=0)
        second = jnp.concatenate(sums[1::2], axis=0)
        low = low_half(first.shape)
        packed = jnp.where(low, first, second)
        packed = packed + pltpu.roll(jnp.where(low, second, first), COLS, 1)
        return jnp.concatenate([packed, jnp.zeros((8 - packed.shape[0], LANES), f32)], axis=0)

    def sum_start(n, payload):
        sum_send[n] = payload
        sum_group[n, group] = payload
        for target in near_group:
            remote(
                sum_send.at[n], sum_group.at[n, group], g_ssem.at[n], g_rsem.at[n], target
            ).start()

    def sum_middle(n):
        all_but_one(sum_group.at[n], ng, g_rsem.at[n]).wait()
        partial = jnp.sum(sum_group[n], axis=0)
        tot_send[n] = partial
        sum_bulk[n, bulk] = partial
        for target in far_bulk:
            remote(tot_send.at[n], sum_bulk.at[n, bulk], b_ssem.at[n], b_rsem.at[n], target).start()

    def sum_finish(n, count):
        all_but_one(sum_bulk.at[n], nb, b_rsem.at[n]).wait()
        total = jnp.sum(sum_bulk[n], axis=0)
        swapped = pltpu.roll(total, COLS, 1)
        halves = (jnp.where(low8, total, swapped), jnp.where(low8, swapped, total))
        return [
            jnp.broadcast_to(halves[i % 2][i // 2 : i // 2 + 1], (8, LANES)) for i in range(count)
        ]

    def scaled(factor, value):
        return (factor * value.reshape(8, 8, LANES)).reshape(NS, LANES)

    coarse_residual(0, k0)
    pl.semaphore_wait(barrier, ng + nb - 2)
    coarse_push(0)
    weight_copies = edge_copies(wtab, wnb_x, wnb_y, ITERS)
    for copy in weight_copies:
        copy.start()

    for copy in prec_loads:
        copy.wait()
    halos0 = local_part(0, k0)

    for copy in inv_loads:
        copy.wait()
    turned = inv_raw[...]
    in_half = (lax.broadcasted_iota(jnp.int32, turned.shape, 1) & (rows - 1)) < rows // 2
    turned = jnp.concatenate(
        [jnp.where(in_half, turned, 0.0), jnp.where(in_half, 0.0, turned)], axis=0
    )
    high, low = split_hi_lo(turned)
    inv_rows[0 : 2 * rows] = high
    inv_rows[2 * rows :] = low

    for copy in diag_loads:
        copy.wait()

    def turn_diag(p, carry):
        both = diag_raw[p].astype(f32)
        diag_t[p, 0:NS] = jnp.transpose(both[:NS]).astype(bf16)
        diag_t[p, NS : 2 * NS] = jnp.transpose(both[NS:]).astype(bf16)
        return carry

    loop(PAIRS, turn_diag)

    small_loads[1].wait()
    small_loads[2].wait()
    face_of = lax.broadcasted_iota(jnp.int32, (CY, 4 * NS), 1) // NS
    cell_y = lax.broadcasted_iota(jnp.int32, (CY, 4 * NS), 0)
    for x in range(CX):
        opened = jnp.transpose(face_ref[x].astype(f32))
        mask = jnp.zeros((CY, 4 * NS), f32)
        for f in range(4):
            mask = jnp.where(face_of == f, opened[:, f : f + 1], mask)
        if x == 0:
            mask = jnp.where((face_of == 0) & (bulk == 0), 0.0, mask)
        if x == CX - 1:
            mask = jnp.where((face_of == 1) & (bulk == nb - 1), 0.0, mask)
        mask = jnp.where((face_of == 2) & (cell_y == 0) & (group == 0), 0.0, mask)
        mask = jnp.where((face_of == 3) & (cell_y == CY - 1) & (group == ng - 1), 0.0, mask)
        value = coup_ref[x] * mask
        first = value.astype(bf16).astype(f32)
        second = (value - first).astype(bf16).astype(f32)
        third = value - first - second
        spread_rows = jnp.transpose(jnp.concatenate([first, second, third], axis=0)).astype(bf16)

        def expand(yy, carry):
            row = lax.broadcasted_iota(jnp.int32, (3 * CY, LANES), 0) & (CY - 1)
            lane = lax.broadcasted_iota(jnp.int32, (3 * CY, LANES), 1)
            pick = jnp.where(row == yy + jnp.where(lane < COLS, 0, HALF), 1.0, 0.0).astype(bf16)
            wide = mm(spread_rows, pick)
            for f in range(4):
                coef[x * HALF + yy, f] = wide[f * NS : (f + 1) * NS]
            return carry

        loop(HALF, expand)

    cors0 = coarse_solve(0)
    own_z(0)
    own_image(0)
    for copy in weight_copies:
        copy.wait_recv()
    wait_edges(0, halos0, cors0)

    def tail0(p, value):
        w0[p] = value
        start = k0[p]
        return ((start, start), (start, value), (value, value))

    payload = sweep(0, tail0, 3)

    coarse_residual(1, w0)
    coarse_push(1)
    halos1 = local_part(1, w0)
    sum_start(0, payload)
    cors1 = coarse_solve(1)
    own_z(1)
    own_image(1)
    wait_edges(1, halos1, cors1)

    def tail1(p, value):
        w1[p] = value
        return ()

    sweep(1, tail1, 0)

    coarse_residual(2, w1)
    coarse_push(2)
    halos2 = local_part(2, w1)
    sum_middle(0)
    cors2 = coarse_solve(2)
    own_z(2)
    own_image(2)
    sum_kk, sum_kw, sum_ww = sum_finish(0, 3)
    beta = jnp.sqrt(sum_kk + tiny_eps)
    s0 = 1.0 / beta
    h00 = sum_kw * s0 * s0
    g00 = sum_kk * s0 * s0
    ww0 = sum_ww * s0 * s0
    h10u = jnp.sqrt(jnp.maximum(ww0 - h00 * h00 * (2.0 - g00), 0.0) + tiny_eps)
    c1 = s0 / h10u
    c2 = h00 * c1
    wait_edges(2, halos2, cors2)

    def tail2(p, value):
        start = k0[p]
        raw0 = w0[p]
        raw1 = w1[p]
        vec1 = scaled(c1, raw0) - scaled(c2, start)
        image1 = scaled(c1, raw1) - scaled(c2, raw0)
        image2 = scaled(c1, value) - scaled(c2, raw1)
        return (
            (start, vec1),
            (vec1, vec1),
            (start, image1),
            (vec1, image1),
            (image1, image1),
            (start, image2),
            (vec1, image2),
            (image1, image2),
            (image2, image2),
        )

    payload = sweep(2, tail2, 9)
    sum_start(1, payload)
    sum_middle(1)
    d_01, d_11, d_0w, d_1w, d_ww, d_0v, d_1v, d_wv, d_vv = sum_finish(1, 9)

    h10 = jnp.sqrt(h10u * h10u * d_11 + tiny_eps)
    t1 = h10u / h10
    t1s = t1 * t1
    g01 = d_01 * s0 * t1
    g11 = d_11 * t1s
    h01 = d_0w * s0 * t1
    h11 = d_1w * t1s
    ww1 = d_ww * t1s
    n1 = ww1 - h01 * h01 * (2.0 - g00) - h11 * h11 * (2.0 - g11) + 2.0 * h01 * h11 * g01
    n1 = jnp.maximum(n1, 0.0)
    h21 = jnp.sqrt(n1 + tiny_eps)
    i21 = 1.0 / h21
    v0 = d_0v * s0 * t1
    v1 = d_1v * t1s
    vw = d_wv * t1s
    vv = d_vv * t1s
    k1w0 = h00 * g01 + h10 * g11
    w1w0 = h00 * h01 + h10 * h11
    vw0 = h00 * v0 + h10 * v1
    h02 = (v0 - h01 * h00 - h11 * h01) * i21
    h12 = (v1 - h01 * k1w0 - h11 * h11) * i21
    w1w2 = (vw - h01 * w1w0 - h11 * ww1) * i21
    h22 = (w1w2 - h01 * h02 - h11 * h12) * i21
    ww2 = vv + h01 * h01 * ww0 + h11 * h11 * ww1
    ww2 = (ww2 - 2.0 * (h01 * vw0 + h11 * vw - h01 * h11 * w1w0)) * i21 * i21
    g02 = (h01 - h01 * g00 - h11 * g01) * i21
    g12 = (h11 - h01 * g01 - h11 * g11) * i21
    g22 = n1 * i21 * i21
    n2 = ww2 - h02 * h02 * (2.0 - g00) - h12 * h12 * (2.0 - g11) - h22 * h22 * (2.0 - g22)
    n2 = n2 + 2.0 * (h02 * h12 * g01 + h02 * h22 * g02 + h12 * h22 * g12)
    h32 = jnp.sqrt(jnp.maximum(n2, 0.0) + tiny_eps)
    y0, y1, y2 = givens_solve([[h00, h10], [h01, h11, h21], [h02, h12, h22, h32]], beta)

    over = y2 * i21
    on1 = y1 - over * h11
    a2 = over * t1 * c1
    a1 = on1 * t1 * c1 - over * t1 * c2
    a0 = y0 * s0 - over * h01 * s0 - on1 * t1 * c2

    def finish(p, carry):
        x = p // HALF
        yy = p % HALF
        total = (
            scaled(a0, zs[0, p].astype(f32))
            + scaled(a1, zs[1, p].astype(f32))
            + scaled(a2, zs[2, p].astype(f32))
        )
        out_ref[x, yy] = total[:, :COLS].astype(bf16)
        out_ref[x, yy + HALF] = pltpu.roll(total, COLS, 1)[:, :COLS].astype(bf16)
        return carry

    loop(PAIRS, finish)

    for step, copies in enumerate((halos0 + cors0, halos1 + cors1, halos2 + cors2)):
        all_but_one(res_buf.at[step], ng, res_ssem.at[step]).wait()
        for copy in copies:
            copy.wait_send()
    for copy in weight_copies:
        copy.wait_send()
    for n in range(2):
        all_but_one(sum_group.at[n], ng, g_ssem.at[n]).wait()
        all_but_one(sum_bulk.at[n], nb, b_ssem.at[n]).wait()


def body(nb, ng, rhs, diag_blocks, precond_blocks, coupling, face_open, agg_id, coarse_basis, coarse_inv):
    rows = AGGS * COMPS
    inverse = jnp.swapaxes(coarse_inv[0], 0, 1)
    any_spec = pl.BlockSpec(memory_space=pl.ANY)
    vmem_spec = pl.BlockSpec(memory_space=pltpu.VMEM)
    smem_spec = pl.BlockSpec(memory_space=pltpu.SMEM)
    field = pltpu.VMEM((PAIRS, NS, LANES), f32)
    dma = pltpu.SemaphoreType.DMA
    return pl.pallas_call(
        functools.partial(kernel, nb, ng),
        out_shape=jax.ShapeDtypeStruct(rhs.shape, bf16),
        in_specs=[any_spec, any_spec, any_spec, any_spec, any_spec, smem_spec, any_spec, any_spec],
        out_specs=vmem_spec,
        scratch_shapes=[
            pltpu.VMEM((CX, CY, 4 * NS), f32),
            pltpu.VMEM((CX, 4, CY), jnp.int32),
            pltpu.VMEM((COMPS, NS), f32),
            pltpu.VMEM((CX, CY, NS, COLS), bf16),
            pltpu.VMEM((PAIRS, 2 * NS, NS), bf16),
            pltpu.VMEM((PAIRS, 2 * NS, NS), bf16),
            pltpu.VMEM((PAIRS, 2 * NS, NS), bf16),
            pltpu.VMEM((rows, ng * rows), f32),
            pltpu.VMEM((4 * rows, ng * rows), bf16),
            pltpu.VMEM((PAIRS, 4, NS, LANES), f32),
            pltpu.VMEM((PAIRS, 8, LANES), f32),
            pltpu.VMEM((2, 2 * COMPS, NS), bf16),
            pltpu.VMEM((NS, 3 * COMPS), bf16),
            field,
            field,
            field,
            field,
            pltpu.VMEM((ITERS, PAIRS, NS, LANES), bf16),
            pltpu.VMEM((ITERS, PAIRS, NS, LANES), bf16),
            pltpu.VMEM((5, AGGS, NS, LANES), f32),
            pltpu.VMEM((ITERS, rows // 2, LANES), bf16),
            pltpu.VMEM((ITERS, ng, rows // 2, LANES), bf16),
            pltpu.VMEM((ITERS, rows // 2, LANES), f32),
            pltpu.VMEM((ITERS, 4, rows // 2, LANES), f32),
            pltpu.VMEM((ITERS, CX, HALF, NS, LANES), bf16),
            pltpu.VMEM((ITERS, CX, 2, NS, LANES), bf16),
            pltpu.VMEM((CX, HALF, 8, LANES), f32),
            pltpu.VMEM((CX, 2, 8, LANES), f32),
            pltpu.VMEM((2, 8, LANES), f32),
            pltpu.VMEM((2, ng, 8, LANES), f32),
            pltpu.VMEM((2, 8, LANES), f32),
            pltpu.VMEM((2, nb, 8, LANES), f32),
            dma((13,)),
            dma((ITERS,)),
            dma((ITERS,)),
            dma((ITERS, 4)),
            dma((ITERS, 4)),
            dma((ITERS + 1, CX)),
            dma((ITERS + 1, CX)),
            dma((ITERS + 1, CX, 2)),
            dma((ITERS + 1, CX, 2)),
            dma((2,)),
            dma((2,)),
            dma((2,)),
            dma((2,)),
        ],
        compiler_params=pltpu.CompilerParams(
            collective_id=0, has_side_effects=True, vmem_limit_bytes=60 * 1024 * 1024
        ),
        cost_estimate=pl.CostEstimate(flops=200_000_000, bytes_accessed=3_000_000, transcendentals=0),
    )(
        rhs,
        diag_blocks,
        precond_blocks,
        coupling,
        jnp.swapaxes(face_open, 1, 2),
        agg_id,
        jnp.swapaxes(coarse_basis, 0, 1),
        inverse,
    )


def solution(mesh):
    in_specs = (
        P("bulk", "group", None, None),
        P("bulk", "group", None, None),
        P("bulk", "group", None, None),
        P("bulk", "group", None),
        P("bulk", "group", None),
        P("bulk", "group"),
        P(),
        P("bulk", None, "group"),
    )
    out_specs = P("bulk", "group", None, None)
    return jax.shard_map(
        functools.partial(body, mesh.shape["bulk"], mesh.shape["group"]),
        mesh=mesh,
        in_specs=in_specs,
        out_specs=out_specs,
        check_vma=False,
    )
```

time: 74.1 us -> 62.7 us (0.85)
  Pallas kernels: 72.1 us -> 60.6 us
    pallas_call x1, Pallas kernels: 72.1 us -> 60.6 us  [body(): pl.pallas_call(functools.partial(kernel, nb, ng), out_shape=jax.ShapeDtyp...]
where the time goes in v3:
time: 62.7 us; the launch traced here: 62.5 us
  Pallas kernels  60.6 us (97%)
  local copies, waits for them, and re-layouts  1.87 us (3%)
    pallas_call x1, Pallas kernels, body(): pl.pallas_call(functools.partial(kernel, nb, ng), out_shape=jax.ShapeDtyp...  60.6 us
    unnamed x1, local copies, waits for them, and re-layouts  1.87 us

profile of v3, /device:TPU:1, one launch (start us, length us, event | category | flops | bytes accessed | tf_op | source)
XLA Modules:
  0.0 62.5 jit_solution(650393711895835724)
XLA Ops:
  0.0 60.6 %shard_map.82 = bf16[2,16,64,64]{3,2,1,0:T(8,128)(2,1)} custom-call(bf16[2,16,64,64]{3,2,1,0:T(8,128)(2,1)} %rhs_hbm.1, bf16[2,16,64,64]{3,2,1,0:T(8,128)(2,1)} %diag_hbm.1, bf16[2,16,64,64]{3,2,1,0:T(8,128)(2,1)} %prec_hbm.1, f32[2,16,256]{2,1,0:T(8,128)} %coup_hbm.1, s32[2,4,16]{2,1,0:T(4,128)} %bitcast.6, s32[2,16]{1,0:T(2,128)} %agg_ref.1, ...), custom_call_target="tpu_custom_call" | custom-call | flops 200000000 | bytes 3000000 | tf_op jit(solution)/shard_map/pallas_call | solution.py:667
  60.6 1.9 %copy.10 = bf16[2,16,64,64]{3,2,1,0:T(8,128)(2,1)} copy(bf16[2,16,64,64]{3,2,1,0:T(8,128)(2,1)} %shard_map.82) | data formatting | bytes 524288

commit v4 on v3

--- a/solution.py
+++ b/solution.py
@@ -111,12 +111,13 @@
     prec_hbm,
     coup_hbm,
     face_hbm,
-    agg_ref,
+    agg_hbm,
     basis_hbm,
     inv_hbm,
     out_ref,
     coup_ref,
     face_ref,
+    agg_ref,
     basis_ref,
     rhs_raw,
     prec,
@@ -183,6 +184,7 @@
         pltpu.make_async_copy(basis_hbm, basis_ref, load_sem.at[10]),
         pltpu.make_async_copy(face_hbm, face_ref, load_sem.at[11]),
         pltpu.make_async_copy(coup_hbm, coup_ref, load_sem.at[12]),
+        pltpu.make_async_copy(agg_hbm, agg_ref, load_sem.at[13]),
     ]
     for copy in loads + small_loads + prec_loads + inv_loads + diag_loads:
         copy.start()
@@ -208,6 +210,7 @@
         wtab[p] = jnp.where(cell == row8, 1.0, 0.0).astype(f32)
         return carry
 
+    small_loads[3].wait()
     loop(PAIRS, make_weights)
 
     weight_scale = (AGGS / (CX * CY)) ** 0.5
@@ -542,6 +545,7 @@
     cors1 = coarse_solve(1)
     own_z(1)
     own_image(1)
+    sum_middle(0)
     wait_edges(1, halos1, cors1)
 
     def tail1(p, value):
@@ -553,7 +557,6 @@
     coarse_residual(2, w1)
     coarse_push(2)
     halos2 = local_part(2, w1)
-    sum_middle(0)
     cors2 = coarse_solve(2)
     own_z(2)
     own_image(2)
@@ -659,19 +662,19 @@
 def body(nb, ng, rhs, diag_blocks, precond_blocks, coupling, face_open, agg_id, coarse_basis, coarse_inv):
     rows = AGGS * COMPS
     inverse = jnp.swapaxes(coarse_inv[0], 0, 1)
-    any_spec = pl.BlockSpec(memory_space=pl.ANY)
+    hbm_spec = pl.BlockSpec(memory_space=pltpu.HBM)
     vmem_spec = pl.BlockSpec(memory_space=pltpu.VMEM)
-    smem_spec = pl.BlockSpec(memory_space=pltpu.SMEM)
     field = pltpu.VMEM((PAIRS, NS, LANES), f32)
     dma = pltpu.SemaphoreType.DMA
-    return pl.pallas_call(
+    call = pl.pallas_call(
         functools.partial(kernel, nb, ng),
         out_shape=jax.ShapeDtypeStruct(rhs.shape, bf16),
-        in_specs=[any_spec, any_spec, any_spec, any_spec, any_spec, smem_spec, any_spec, any_spec],
+        in_specs=[hbm_spec] * 8,
         out_specs=vmem_spec,
         scratch_shapes=[
             pltpu.VMEM((CX, CY, 4 * NS), f32),
             pltpu.VMEM((CX, 4, CY), jnp.int32),
+            pltpu.SMEM((CX, CY), jnp.int32),
             pltpu.VMEM((COMPS, NS), f32),
             pltpu.VMEM((CX, CY, NS, COLS), bf16),
             pltpu.VMEM((PAIRS, 2 * NS, NS), bf16),
@@ -702,7 +705,7 @@
             pltpu.VMEM((2, ng, 8, LANES), f32),
             pltpu.VMEM((2, 8, LANES), f32),
             pltpu.VMEM((2, nb, 8, LANES), f32),
-            dma((13,)),
+            dma((14,)),
             dma((ITERS,)),
             dma((ITERS,)),
             dma((ITERS, 4)),
@@ -717,10 +720,11 @@
             dma((2,)),
         ],
         compiler_params=pltpu.CompilerParams(
-            collective_id=0, has_side_effects=True, vmem_limit_bytes=60 * 1024 * 1024
+            collective_id=0, has_side_effects=True, vmem_limit_bytes=32 * 1024 * 1024
         ),
         cost_estimate=pl.CostEstimate(flops=200_000_000, bytes_accessed=3_000_000, transcendentals=0),
-    )(
+    )
+    operands = (
         rhs,
         diag_blocks,
         precond_blocks,
@@ -730,6 +734,7 @@
         jnp.swapaxes(coarse_basis, 0, 1),
         inverse,
     )
+    return call(*[pltpu.with_memory_space_constraint(x, pltpu.HBM) for x in operands])
 
 
 def solution(mesh):

time: 62.7 us -> 58.5 us (0.933)
  Pallas kernels: 60.6 us -> 57.6 us
  local copies, waits for them, and re-layouts: 1.87 us -> 0.8 us
    pallas_call x1, Pallas kernels: 60.6 us -> 57.6 us  [body(): call(*[pltpu.with_memory_space_constraint(x, pltpu.HBM) for x in operands])]
    unnamed x1, local copies, waits for them, and re-layouts: 1.87 us -> 0.8 us
where the time goes in v4:
time: 58.5 us; the launch traced here: 58.4 us
  Pallas kernels  57.6 us (98%)
  local copies, waits for them, and re-layouts  0.8 us (1%)
    pallas_call x1, Pallas kernels, body(): call(*[pltpu.with_memory_space_constraint(x, pltpu.HBM) for x in operands])  57.6 us

profile of v4, /device:TPU:1, one launch (start us, length us, event | category | flops | bytes accessed | tf_op | source)
XLA Modules:
  0.0 58.4 jit_solution(3550835075017167927)
XLA Ops:
  0.0 57.6 %shard_map.82 = bf16[2,16,64,64]{3,2,1,0:T(8,128)(2,1)S(1)} custom-call(bf16[2,16,64,64]{3,2,1,0:T(8,128)(2,1)} %rhs_hbm.1, bf16[2,16,64,64]{3,2,1,0:T(8,128)(2,1)} %diag_hbm.1, bf16[2,16,64,64]{3,2,1,0:T(8,128)(2,1)} %prec_hbm.1, f32[2,16,256]{2,1,0:T(8,128)} %coup_hbm.1, s32[2,4,16]{2,1,0:T(4,128)} %bitcast.6, s32[2,16]{1,0:T(2,128)} %agg_hbm.1, ...), custom_call_target="tpu_custom_call" | custom-call | flops 200000000 | bytes 3000000 | tf_op jit(solution)/shard_map/pallas_call | solution.py:737
  57.6 0.8 %copy.10 = bf16[2,16,64,64]{3,2,1,0:T(8,128)(2,1)} copy(bf16[2,16,64,64]{3,2,1,0:T(8,128)(2,1)S(1)} %shard_map.82) | data formatting | bytes 524288

commit v5 on v4

--- a/solution.py
+++ b/solution.py
@@ -71,35 +71,30 @@
 
 
 def givens_solve(hessen_cols, beta_norm):
-    cosine_list = []
-    sine_list = []
+    rotations = []
     target = [beta_norm] + [jnp.zeros_like(beta_norm) for _ in range(ITERS)]
     triangle = []
     for section in range(ITERS):
         column = list(hessen_cols[section])
-        for earlier in range(section):
+        for earlier, (cosine, sine, _) in enumerate(rotations):
             upper = column[earlier]
             lower = column[earlier + 1]
-            column[earlier] = cosine_list[earlier] * upper + sine_list[earlier] * lower
-            column[earlier + 1] = -sine_list[earlier] * upper + cosine_list[earlier] * lower
+            column[earlier] = cosine * upper + sine * lower
+            column[earlier + 1] = cosine * lower - sine * upper
         upper = column[section]
         lower = column[section + 1]
-        radius = jnp.sqrt(upper * upper + lower * lower)
-        cosine = upper / radius
-        sine_val = lower / radius
-        cosine_list.append(cosine)
-        sine_list.append(sine_val)
-        column[section] = radius
+        inverse = lax.rsqrt(upper * upper + lower * lower)
+        rotations.append((upper * inverse, lower * inverse, inverse))
         carried = target[section]
-        target[section] = cosine * carried
-        target[section + 1] = -sine_val * carried
-        triangle.append(column[: section + 1])
+        target[section] = rotations[-1][0] * carried
+        target[section + 1] = -rotations[-1][1] * carried
+        triangle.append(column[:section])
     result = [None] * ITERS
     for section in reversed(range(ITERS)):
         accumulated = target[section]
         for later in range(section + 1, ITERS):
             accumulated = accumulated - triangle[later][section] * result[later]
-        result[section] = accumulated / triangle[section][section]
+        result[section] = accumulated * rotations[section][2]
     return result
 
 
@@ -186,8 +181,7 @@
         pltpu.make_async_copy(coup_hbm, coup_ref, load_sem.at[12]),
         pltpu.make_async_copy(agg_hbm, agg_ref, load_sem.at[13]),
     ]
-    for copy in loads + small_loads + prec_loads + inv_loads + diag_loads:
-        copy.start()
+    loads[0].start()
 
     barrier = pltpu.get_barrier_semaphore()
 
@@ -195,6 +189,8 @@
     far_bulk = far_targets(nb, bulk)
     for target in near_group + far_bulk:
         pl.semaphore_signal(barrier, inc=1, device_id=target, device_id_type=pl.DeviceIdType.MESH)
+    for copy in small_loads + prec_loads + inv_loads + diag_loads:
+        copy.start()
 
     rows = AGGS * COMPS
     low8 = low_half((8, LANES))
@@ -220,8 +216,8 @@
     stacked = jnp.concatenate([high.astype(f32), high.astype(f32), low.astype(f32)], axis=0)
     bas_w[...] = jnp.transpose(stacked).astype(bf16)
     high, low = split_hi_lo(turned * weight_scale)
-    bas_t[0] = jnp.concatenate([high, high], axis=0)
-    bas_t[1] = jnp.concatenate([low, low], axis=0)
+    stacked = jnp.concatenate([high.astype(f32), high.astype(f32), low.astype(f32)], axis=1)
+    bas_t[...] = jnp.concatenate([stacked, stacked], axis=0).astype(bf16)
 
     loads[0].wait()
 
@@ -255,16 +251,17 @@
 
         zero = jnp.zeros((8, 8, LANES), f32)
         sums = loop(PAIRS, add, (zero,) * AGGS)
-        sums = [s.reshape(NS, LANES) for s in sums]
-        parts = []
+        project(step, [s.reshape(NS, LANES) for s in sums])
+
+    def project(step, sums):
+        totals = []
         for kl in range(2):
             keep = jnp.where(low64, sums[kl], sums[kl + 2])
             move = jnp.where(low64, sums[kl + 2], sums[kl])
-            total = keep + pltpu.roll(move, COLS, 1)
-            high, low = split_hi_lo(total)
-            part = mm(bas_t[0], high) + mm(bas_t[0], low) + mm(bas_t[1], high)
-            parts.append(part[:COMPS])
-        res = jnp.concatenate(parts, axis=0).astype(bf16)
+            totals.append(keep + pltpu.roll(move, COLS, 1))
+        high, low = split_hi_lo(jnp.concatenate(totals, axis=1))
+        part = mm(bas_t[...], jnp.concatenate([high, low, high], axis=0))[:COMPS]
+        res = jnp.concatenate([part[:, :LANES], part[:, LANES:]], axis=0).astype(bf16)
         res_send[step] = res
         res_buf[step, group] = res
 
@@ -387,9 +384,10 @@
         loop(PAIRS, one)
 
     def wait_edges(step, halos, cors):
-        for n in range(4):
+        for copy in halos:
+            copy.wait_recv()
+        for n in (2, 3, 0, 1):
             cors[n].wait_recv()
-        for n in range(4):
             got = cor_buf[step, n]
             swapped = pltpu.roll(got, COLS, 1)
             make_spread(
@@ -398,30 +396,58 @@
                     [jnp.where(low16, got, swapped), jnp.where(low16, swapped, got)], axis=0
                 ),
             )
-        for copy in halos:
-            copy.wait_recv()
-
-    def sweep(step, tail, count):
+
+    def add_terms(sums, terms):
+        return [
+            s + jnp.sum((a * b).reshape(-1, 8, LANES), axis=0) for s, (a, b) in zip(sums, terms)
+        ]
+
+    def sweep(step, tail, count, weight=None, next_step=None):
         sums = [jnp.zeros((8, LANES), f32)] * count
-        for p in range(PAIRS):
-            x = p // HALF
-            yy = p % HALF
-            beside = joined(x, wnb_x[x, yy], halo_x[step, x, yy]).astype(f32)
-            value = acc[p] - coef[p, x] * beside
-            if yy == 0:
-                got = joined(2, wnb_y[x, 0], halo_y[step, x, 0]).astype(f32)
-                own = zs[step, p + HALF - 1].astype(f32)
-                value = value - coef[p, 2] * pltpu.roll(jnp.where(low64, own, got), COLS, 1)
-            if yy == HALF - 1:
-                got = joined(3, wnb_y[x, 1], halo_y[step, x, 1]).astype(f32)
-                own = zs[step, p - HALF + 1].astype(f32)
-                value = value - coef[p, 3] * pltpu.roll(jnp.where(low64, got, own), COLS, 1)
-            terms = tail(p, value)
-            sums = [
-                s + jnp.sum((a * b).reshape(8, 8, LANES), axis=0) for s, (a, b) in zip(sums, terms)
-            ]
-        if not sums:
-            return None
+        chunk = 16
+        low = low_half((chunk, LANES))
+        chunks = []
+        for start in range(0, NS, chunk):
+            part = pl.ds(start, chunk)
+            held = [[spread[n, k, part] for k in range(AGGS)] for n in range(2)]
+            cells = [jnp.zeros((chunk, LANES), f32)] * AGGS
+
+            def whole(n, weights, local):
+                total = local.astype(f32)
+                for k in range(AGGS):
+                    total = total + weights[k : k + 1] * (held[n][k] if n < 2 else spread[n, k, part])
+                return total.astype(bf16).astype(f32)
+
+            for p in range(PAIRS):
+                x = p // HALF
+                yy = p % HALF
+                value = coef[p, x, part] * whole(x, wnb_x[x, yy], halo_x[step, x, yy, part])
+                if yy == 0:
+                    got = whole(2, wnb_y[x, 0], halo_y[step, x, 0, part])
+                    own = zs[step, p + HALF - 1, part].astype(f32)
+                    moved = pltpu.roll(jnp.where(low, own, got), COLS, 1)
+                    value = value + coef[p, 2, part] * moved
+                if yy == HALF - 1:
+                    got = whole(3, wnb_y[x, 1], halo_y[step, x, 1, part])
+                    own = zs[step, p - HALF + 1, part].astype(f32)
+                    moved = pltpu.roll(jnp.where(low, got, own), COLS, 1)
+                    value = value + coef[p, 3, part] * moved
+                if weight is not None:
+                    value = scaled(weight, value)
+                value = acc[p, part] - value
+                sums = add_terms(sums, tail(p, part, value))
+                if next_step is not None:
+                    cells = [cells[k] + wtab[p, k : k + 1] * value for k in range(AGGS)]
+            chunks.append(cells)
+        if next_step is not None:
+            project(
+                next_step,
+                [jnp.concatenate([c[k] for c in chunks], axis=0) for k in range(AGGS)],
+            )
+        return sums
+
+    def pack_sums(sums):
+        count = len(sums)
         sums = [jnp.sum(s, axis=0, keepdims=True) for s in sums]
         sums += [sums[-1]] * (count % 2)
         first = jnp.concatenate(sums[0::2], axis=0)
@@ -457,7 +483,7 @@
         ]
 
     def scaled(factor, value):
-        return (factor * value.reshape(8, 8, LANES)).reshape(NS, LANES)
+        return (factor * value.reshape(-1, 8, LANES)).reshape(value.shape)
 
     coarse_residual(0, k0)
     pl.semaphore_wait(barrier, ng + nb - 2)
@@ -531,15 +557,15 @@
         copy.wait_recv()
     wait_edges(0, halos0, cors0)
 
-    def tail0(p, value):
-        w0[p] = value
-        start = k0[p]
+    def tail0(p, part, value):
+        w0[p, part] = value
+        start = k0[p, part]
         return ((start, start), (start, value), (value, value))
 
-    payload = sweep(0, tail0, 3)
-
-    coarse_residual(1, w0)
+    sums = sweep(0, tail0, 3, next_step=1)
+
     coarse_push(1)
+    payload = pack_sums(sums)
     halos1 = local_part(1, w0)
     sum_start(0, payload)
     cors1 = coarse_solve(1)
@@ -548,13 +574,12 @@
     sum_middle(0)
     wait_edges(1, halos1, cors1)
 
-    def tail1(p, value):
-        w1[p] = value
+    def tail1(p, part, value):
+        w1[p, part] = value
         return ()
 
-    sweep(1, tail1, 0)
-
-    coarse_residual(2, w1)
+    sweep(1, tail1, 0, next_step=2)
+
     coarse_push(2)
     halos2 = local_part(2, w1)
     cors2 = coarse_solve(2)
@@ -569,34 +594,50 @@
     h10u = jnp.sqrt(jnp.maximum(ww0 - h00 * h00 * (2.0 - g00), 0.0) + tiny_eps)
     c1 = s0 / h10u
     c2 = h00 * c1
-    wait_edges(2, halos2, cors2)
-
-    def tail2(p, value):
+
+    early = [jnp.zeros((8, LANES), f32)] * 5
+    for p in range(PAIRS):
         start = k0[p]
         raw0 = w0[p]
         raw1 = w1[p]
         vec1 = scaled(c1, raw0) - scaled(c2, start)
         image1 = scaled(c1, raw1) - scaled(c2, raw0)
-        image2 = scaled(c1, value) - scaled(c2, raw1)
+        acc[p] = scaled(c1, acc[p]) - scaled(c2, raw1)
+        w0[p] = vec1
+        w1[p] = image1
+        early = add_terms(
+            early,
+            ((start, vec1), (vec1, vec1), (start, image1), (vec1, image1), (image1, image1)),
+        )
+    wait_edges(2, halos2, cors2)
+
+    def tail2(p, part, image2):
         return (
-            (start, vec1),
-            (vec1, vec1),
-            (start, image1),
-            (vec1, image1),
-            (image1, image1),
-            (start, image2),
-            (vec1, image2),
-            (image1, image2),
+            (k0[p, part], image2),
+            (w0[p, part], image2),
+            (w1[p, part], image2),
             (image2, image2),
         )
 
-    payload = sweep(2, tail2, 9)
-    sum_start(1, payload)
+    late = sweep(2, tail2, 4, c1)
+    sum_start(1, pack_sums(early + late))
+
+    for copies in (weight_copies, halos0 + cors0, halos1 + cors1, halos2 + cors2):
+        for copy in copies:
+            copy.wait_send()
+    for step in range(ITERS):
+        all_but_one(res_buf.at[step], ng, res_ssem.at[step]).wait()
+    all_but_one(sum_group.at[0], ng, g_ssem.at[0]).wait()
+    all_but_one(sum_bulk.at[0], nb, b_ssem.at[0]).wait()
+
     sum_middle(1)
+    all_but_one(sum_group.at[1], ng, g_ssem.at[1]).wait()
     d_01, d_11, d_0w, d_1w, d_ww, d_0v, d_1v, d_wv, d_vv = sum_finish(1, 9)
 
-    h10 = jnp.sqrt(h10u * h10u * d_11 + tiny_eps)
-    t1 = h10u / h10
+    h10_sq = h10u * h10u * d_11 + tiny_eps
+    i10 = lax.rsqrt(h10_sq)
+    h10 = h10_sq * i10
+    t1 = h10u * i10
     t1s = t1 * t1
     g01 = d_01 * s0 * t1
     g11 = d_11 * t1s
@@ -605,8 +646,8 @@
     ww1 = d_ww * t1s
     n1 = ww1 - h01 * h01 * (2.0 - g00) - h11 * h11 * (2.0 - g11) + 2.0 * h01 * h11 * g01
     n1 = jnp.maximum(n1, 0.0)
-    h21 = jnp.sqrt(n1 + tiny_eps)
-    i21 = 1.0 / h21
+    i21 = lax.rsqrt(n1 + tiny_eps)
+    h21 = (n1 + tiny_eps) * i21
     v0 = d_0v * s0 * t1
     v1 = d_1v * t1s
     vw = d_wv * t1s
@@ -648,15 +689,7 @@
 
     loop(PAIRS, finish)
 
-    for step, copies in enumerate((halos0 + cors0, halos1 + cors1, halos2 + cors2)):
-        all_but_one(res_buf.at[step], ng, res_ssem.at[step]).wait()
-        for copy in copies:
-            copy.wait_send()
-    for copy in weight_copies:
-        copy.wait_send()
-    for n in range(2):
-        all_but_one(sum_group.at[n], ng, g_ssem.at[n]).wait()
-        all_but_one(sum_bulk.at[n], nb, b_ssem.at[n]).wait()
+    all_but_one(sum_bulk.at[1], nb, b_ssem.at[1]).wait()
 
 
 def body(nb, ng, rhs, diag_blocks, precond_blocks, coupling, face_open, agg_id, coarse_basis, coarse_inv):
@@ -684,7 +717,7 @@
             pltpu.VMEM((4 * rows, ng * rows), bf16),
             pltpu.VMEM((PAIRS, 4, NS, LANES), f32),
             pltpu.VMEM((PAIRS, 8, LANES), f32),
-            pltpu.VMEM((2, 2 * COMPS, NS), bf16),
+            pltpu.VMEM((2 * COMPS, 3 * NS), bf16),
             pltpu.VMEM((NS, 3 * COMPS), bf16),
             field,
             field,

time: 58.5 us -> 57.6 us (0.985)
  Pallas kernels: 57.6 us -> 56.6 us
    pallas_call x1, Pallas kernels: 57.6 us -> 56.6 us  [body(): call(*[pltpu.with_memory_space_constraint(x, pltpu.HBM) for x in operands])]
where the time goes in v5:
time: 57.6 us; the launch traced here: 57.4 us
  Pallas kernels  56.6 us (98%)
  local copies, waits for them, and re-layouts  0.8 us (1%)
    pallas_call x1, Pallas kernels, body(): call(*[pltpu.with_memory_space_constraint(x, pltpu.HBM) for x in operands])  56.6 us

profile of v5, /device:TPU:1, one launch (start us, length us, event | category | flops | bytes accessed | tf_op | source)
XLA Modules:
  0.0 57.4 jit_solution(3030768854859059912)
XLA Ops:
  0.0 56.6 %shard_map.82 = bf16[2,16,64,64]{3,2,1,0:T(8,128)(2,1)S(1)} custom-call(bf16[2,16,64,64]{3,2,1,0:T(8,128)(2,1)} %rhs_hbm.1, bf16[2,16,64,64]{3,2,1,0:T(8,128)(2,1)} %diag_hbm.1, bf16[2,16,64,64]{3,2,1,0:T(8,128)(2,1)} %prec_hbm.1, f32[2,16,256]{2,1,0:T(8,128)} %coup_hbm.1, s32[2,4,16]{2,1,0:T(4,128)} %bitcast.6, s32[2,16]{1,0:T(2,128)} %agg_hbm.1, ...), custom_call_target="tpu_custom_call" | custom-call | flops 200000000 | bytes 3000000 | tf_op jit(solution)/shard_map/pallas_call | solution.py:770
  56.7 0.8 %copy.10 = bf16[2,16,64,64]{3,2,1,0:T(8,128)(2,1)} copy(bf16[2,16,64,64]{3,2,1,0:T(8,128)(2,1)S(1)} %shard_map.82) | data formatting | bytes 524288

commit v6 on v5

--- a/solution.py
+++ b/solution.py
@@ -131,6 +131,7 @@
     yb,
     zs,
     spread,
+    answers,
     res_send,
     res_buf,
     cor_send,
@@ -251,9 +252,14 @@
 
         zero = jnp.zeros((8, 8, LANES), f32)
         sums = loop(PAIRS, add, (zero,) * AGGS)
-        project(step, [s.reshape(NS, LANES) for s in sums])
-
-    def project(step, sums):
+        keep_residual(step, project([s.reshape(NS, LANES) for s in sums]))
+
+    def keep_residual(step, res):
+        res = res.astype(bf16)
+        res_send[step] = res
+        res_buf[step, group] = res
+
+    def project(sums):
         totals = []
         for kl in range(2):
             keep = jnp.where(low64, sums[kl], sums[kl + 2])
@@ -261,9 +267,7 @@
             totals.append(keep + pltpu.roll(move, COLS, 1))
         high, low = split_hi_lo(jnp.concatenate(totals, axis=1))
         part = mm(bas_t[...], jnp.concatenate([high, low, high], axis=0))[:COMPS]
-        res = jnp.concatenate([part[:, :LANES], part[:, LANES:]], axis=0).astype(bf16)
-        res_send[step] = res
-        res_buf[step, group] = res
+        return jnp.concatenate([part[:, :LANES], part[:, LANES:]], axis=0)
 
     def coarse_push(step):
         for target in near_group:
@@ -383,34 +387,109 @@
 
         loop(PAIRS, one)
 
-    def wait_edges(step, halos, cors):
+    def neighbour_cor(step, n):
+        got = cor_buf[step, n]
+        swapped = pltpu.roll(got, COLS, 1)
+        return jnp.concatenate(
+            [jnp.where(low16, got, swapped), jnp.where(low16, swapped, got)], axis=0
+        )
+
+    def masked_sums(pairs, value_of):
+        chunk = 16
+        chunks = []
+        for start in range(0, NS, chunk):
+            part = pl.ds(start, chunk)
+            cells = [jnp.zeros((chunk, LANES), f32)] * AGGS
+            for p in pairs:
+                value = value_of(p, part)
+                cells = [cells[k] + wtab[p, k : k + 1] * value for k in range(AGGS)]
+            chunks.append(cells)
+        return [jnp.concatenate([c[k] for c in chunks], axis=0) for k in range(AGGS)]
+
+    low_chunk = low_half((16, LANES))
+    ends = [p for p in range(PAIRS) if p % HALF in (0, HALF - 1)]
+
+    def answer_tables():
+        row = lax.broadcasted_iota(jnp.int32, (rows, LANES), 0)
+        lane = lax.broadcasted_iota(jnp.int32, (rows, LANES), 1) & (COLS - 1)
+        for n in range(4):
+            make_spread(n, jnp.where(lane == row + (n % 2) * rows, 1.0, 0.0).astype(f32))
+
+        def only(n, weights, part):
+            total = weights[0:1] * spread[n, 0, part]
+            for k in range(1, AGGS):
+                total = total + weights[k : k + 1] * spread[n, k, part]
+            return total
+
+        def across(p, part):
+            x = p // HALF
+            return -coef[p, x, part] * only(x, wnb_x[x, p % HALF], part)
+
+        def along(p, part):
+            x = p // HALF
+            if p % HALF == 0:
+                got = jnp.where(low_chunk, 0.0, only(2, wnb_y[x, 0], part))
+                return -coef[p, 2, part] * pltpu.roll(got, COLS, 1)
+            got = jnp.where(low_chunk, only(3, wnb_y[x, 1], part), 0.0)
+            return -coef[p, 3, part] * pltpu.roll(got, COLS, 1)
+
+        table = jnp.concatenate(
+            [project(masked_sums(range(PAIRS), across)), project(masked_sums(ends, along))], axis=1
+        )
+        high, low = split_hi_lo(table)
+        answers[...] = jnp.concatenate([high, low], axis=0)
+
+    def early_residual(step):
+        def value_of(p, part):
+            x = p // HALF
+            yy = p % HALF
+            value = acc[p, part] - coef[p, x, part] * halo_x[step, x, yy, part].astype(f32)
+            if yy == 0:
+                got = halo_y[step, x, 0, part].astype(f32)
+                own = zs[step, p + HALF - 1, part].astype(f32)
+                moved = pltpu.roll(jnp.where(low_chunk, own, got), COLS, 1)
+                value = value - coef[p, 2, part] * moved
+            if yy == HALF - 1:
+                got = halo_y[step, x, 1, part].astype(f32)
+                own = zs[step, p - HALF + 1, part].astype(f32)
+                moved = pltpu.roll(jnp.where(low_chunk, got, own), COLS, 1)
+                value = value - coef[p, 3, part] * moved
+            return value
+
+        return project(masked_sums(range(PAIRS), value_of))
+
+    def answered_residual(step, res):
+        blocks = []
+        for n in (0, 2):
+            both = jnp.concatenate([neighbour_cor(step, n), neighbour_cor(step, n + 1)], axis=0)
+            blocks += [jnp.where(low64, both, 0.0), jnp.where(low64, 0.0, both)]
+        added = mm(answers[...], jnp.concatenate(blocks, axis=0).astype(bf16))
+        keep_residual(step + 1, res + added[: rows // 2] + added[rows // 2 :])
+
+    def wait_halos(halos):
         for copy in halos:
             copy.wait_recv()
+
+    def wait_cors(cors):
         for n in (2, 3, 0, 1):
             cors[n].wait_recv()
-            got = cor_buf[step, n]
-            swapped = pltpu.roll(got, COLS, 1)
-            make_spread(
-                n,
-                jnp.concatenate(
-                    [jnp.where(low16, got, swapped), jnp.where(low16, swapped, got)], axis=0
-                ),
-            )
+
+    def spread_neighbours(step):
+        for n in (2, 3, 0, 1):
+            make_spread(n, neighbour_cor(step, n))
 
     def add_terms(sums, terms):
         return [
             s + jnp.sum((a * b).reshape(-1, 8, LANES), axis=0) for s, (a, b) in zip(sums, terms)
         ]
 
-    def sweep(step, tail, count, weight=None, next_step=None):
+    def sweep(step, tail, count, weight=None):
         sums = [jnp.zeros((8, LANES), f32)] * count
         chunk = 16
         low = low_half((chunk, LANES))
-        chunks = []
         for start in range(0, NS, chunk):
             part = pl.ds(start, chunk)
             held = [[spread[n, k, part] for k in range(AGGS)] for n in range(2)]
-            cells = [jnp.zeros((chunk, LANES), f32)] * AGGS
 
             def whole(n, weights, local):
                 total = local.astype(f32)
@@ -436,14 +515,6 @@
                     value = scaled(weight, value)
                 value = acc[p, part] - value
                 sums = add_terms(sums, tail(p, part, value))
-                if next_step is not None:
-                    cells = [cells[k] + wtab[p, k : k + 1] * value for k in range(AGGS)]
-            chunks.append(cells)
-        if next_step is not None:
-            project(
-                next_step,
-                [jnp.concatenate([c[k] for c in chunks], axis=0) for k in range(AGGS)],
-            )
         return sums
 
     def pack_sums(sums):
@@ -455,7 +526,11 @@
         low = low_half(first.shape)
         packed = jnp.where(low, first, second)
         packed = packed + pltpu.roll(jnp.where(low, second, first), COLS, 1)
-        return jnp.concatenate([packed, jnp.zeros((8 - packed.shape[0], LANES), f32)], axis=0)
+        if packed.shape[0] < 4:
+            packed = jnp.concatenate(
+                [packed, jnp.zeros((4 - packed.shape[0], LANES), f32)], axis=0
+            )
+        return packed
 
     def sum_start(n, payload):
         sum_send[n] = payload
@@ -477,7 +552,8 @@
         all_but_one(sum_bulk.at[n], nb, b_rsem.at[n]).wait()
         total = jnp.sum(sum_bulk[n], axis=0)
         swapped = pltpu.roll(total, COLS, 1)
-        halves = (jnp.where(low8, total, swapped), jnp.where(low8, swapped, total))
+        low = low_half((4, LANES))
+        halves = (jnp.where(low, total, swapped), jnp.where(low, swapped, total))
         return [
             jnp.broadcast_to(halves[i % 2][i // 2 : i // 2 + 1], (8, LANES)) for i in range(count)
         ]
@@ -555,32 +631,40 @@
     own_image(0)
     for copy in weight_copies:
         copy.wait_recv()
-    wait_edges(0, halos0, cors0)
+    answer_tables()
+    wait_halos(halos0)
+    res = early_residual(0)
+    wait_cors(cors0)
+    answered_residual(0, res)
+    coarse_push(1)
+    spread_neighbours(0)
 
     def tail0(p, part, value):
         w0[p, part] = value
         start = k0[p, part]
         return ((start, start), (start, value), (value, value))
 
-    sums = sweep(0, tail0, 3, next_step=1)
-
-    coarse_push(1)
-    payload = pack_sums(sums)
+    payload = pack_sums(sweep(0, tail0, 3))
+
     halos1 = local_part(1, w0)
     sum_start(0, payload)
     cors1 = coarse_solve(1)
     own_z(1)
     own_image(1)
     sum_middle(0)
-    wait_edges(1, halos1, cors1)
+    wait_halos(halos1)
+    res = early_residual(1)
+    wait_cors(cors1)
+    answered_residual(1, res)
+    coarse_push(2)
+    spread_neighbours(1)
 
     def tail1(p, part, value):
         w1[p, part] = value
         return ()
 
-    sweep(1, tail1, 0, next_step=2)
-
-    coarse_push(2)
+    sweep(1, tail1, 0)
+
     halos2 = local_part(2, w1)
     cors2 = coarse_solve(2)
     own_z(2)
@@ -595,7 +679,7 @@
     c1 = s0 / h10u
     c2 = h00 * c1
 
-    early = [jnp.zeros((8, LANES), f32)] * 5
+    early = [jnp.zeros((8, LANES), f32)] * 4
     for p in range(PAIRS):
         start = k0[p]
         raw0 = w0[p]
@@ -607,9 +691,11 @@
         w1[p] = image1
         early = add_terms(
             early,
-            ((start, vec1), (vec1, vec1), (start, image1), (vec1, image1), (image1, image1)),
+            ((vec1, vec1), (start, image1), (vec1, image1), (image1, image1)),
         )
-    wait_edges(2, halos2, cors2)
+    wait_halos(halos2)
+    wait_cors(cors2)
+    spread_neighbours(2)
 
     def tail2(p, part, image2):
         return (
@@ -632,7 +718,8 @@
 
     sum_middle(1)
     all_but_one(sum_group.at[1], ng, g_ssem.at[1]).wait()
-    d_01, d_11, d_0w, d_1w, d_ww, d_0v, d_1v, d_wv, d_vv = sum_finish(1, 9)
+    d_11, d_0w, d_1w, d_ww, d_0v, d_1v, d_wv, d_vv = sum_finish(1, 8)
+    d_01 = c1 * sum_kw * (tiny_eps * s0 * s0)
 
     h10_sq = h10u * h10u * d_11 + tiny_eps
     i10 = lax.rsqrt(h10_sq)
@@ -726,6 +813,7 @@
             pltpu.VMEM((ITERS, PAIRS, NS, LANES), bf16),
             pltpu.VMEM((ITERS, PAIRS, NS, LANES), bf16),
             pltpu.VMEM((5, AGGS, NS, LANES), f32),
+            pltpu.VMEM((rows, 2 * LANES), bf16),
             pltpu.VMEM((ITERS, rows // 2, LANES), bf16),
             pltpu.VMEM((ITERS, ng, rows // 2, LANES), bf16),
             pltpu.VMEM((ITERS, rows // 2, LANES), f32),
@@ -734,10 +822,10 @@
             pltpu.VMEM((ITERS, CX, 2, NS, LANES), bf16),
             pltpu.VMEM((CX, HALF, 8, LANES), f32),
             pltpu.VMEM((CX, 2, 8, LANES), f32),
-            pltpu.VMEM((2, 8, LANES), f32),
-            pltpu.VMEM((2, ng, 8, LANES), f32),
-            pltpu.VMEM((2, 8, LANES), f32),
-            pltpu.VMEM((2, nb, 8, LANES), f32),
+            pltpu.VMEM((2, 4, LANES), f32),
+            pltpu.VMEM((2, ng, 4, LANES), f32),
+            pltpu.VMEM((2, 4, LANES), f32),
+            pltpu.VMEM((2, nb, 4, LANES), f32),
             dma((14,)),
             dma((ITERS,)),
             dma((ITERS,)),

time: 57.6 us -> 55.8 us (0.969)
  Pallas kernels: 56.6 us -> 54.8 us
    pallas_call x1, Pallas kernels: 56.6 us -> 54.8 us  [body(): call(*[pltpu.with_memory_space_constraint(x, pltpu.HBM) for x in operands])]
where the time goes in v6:
time: 55.8 us; the launch traced here: 55.7 us
  Pallas kernels  54.8 us (98%)
  local copies, waits for them, and re-layouts  0.8 us (1%)
    pallas_call x1, Pallas kernels, body(): call(*[pltpu.with_memory_space_constraint(x, pltpu.HBM) for x in operands])  54.8 us

profile of v6, /device:TPU:1, one launch (start us, length us, event | category | flops | bytes accessed | tf_op | source)
XLA Modules:
  0.0 55.7 jit_solution(2227625424968747025)
XLA Ops:
  0.0 54.8 %shard_map.82 = bf16[2,16,64,64]{3,2,1,0:T(8,128)(2,1)S(1)} custom-call(bf16[2,16,64,64]{3,2,1,0:T(8,128)(2,1)} %rhs_hbm.1, bf16[2,16,64,64]{3,2,1,0:T(8,128)(2,1)} %diag_hbm.1, bf16[2,16,64,64]{3,2,1,0:T(8,128)(2,1)} %prec_hbm.1, f32[2,16,256]{2,1,0:T(8,128)} %coup_hbm.1, s32[2,4,16]{2,1,0:T(4,128)} %bitcast.6, s32[2,16]{1,0:T(2,128)} %agg_hbm.1, ...), custom_call_target="tpu_custom_call" | custom-call | flops 200000000 | bytes 3000000 | tf_op jit(solution)/shard_map/pallas_call | solution.py:858
  54.9 0.8 %copy.10 = bf16[2,16,64,64]{3,2,1,0:T(8,128)(2,1)} copy(bf16[2,16,64,64]{3,2,1,0:T(8,128)(2,1)S(1)} %shard_map.82) | data formatting | bytes 524288

commit v7 on v6

--- a/solution.py
+++ b/solution.py
@@ -51,18 +51,38 @@
     return sorted(range(1, count), key=lambda d: -min(d, count - d))
 
 
-def far_targets(nb, bulk):
-    along = 8 if nb % 8 == 0 else nb
-    across = nb // along
-
-    def hops(d):
-        high, low = d // along, d % along
-        return min(high, across - high) + min(low, along - low)
-
-    base = (bulk // along) * along
+def along_y(nb):
+    return 8 if nb % 8 == 0 else nb
+
+
+def hops(d, count):
+    return min(d, count - d)
+
+
+def plane_targets(nb, bulk, group):
+    count = along_y(nb)
+    base = (bulk // count) * count
     return [
-        {"bulk": lax.rem(base + (d // along) * along, nb) + lax.rem(bulk + d % along, along)}
-        for d in sorted(range(1, nb), key=lambda d: -hops(d))
+        {
+            "bulk": base + lax.rem(bulk + d % count, count),
+            "group": (group // 2) * 2 + lax.rem(group + d // count, 2),
+        }
+        for d in sorted(range(1, 2 * count), key=lambda d: -hops(d % count, count))
+    ]
+
+
+def cross_targets(nb, ng, bulk, group):
+    count = along_y(nb)
+    across = nb // count
+    deep = ng // 2
+    return [
+        {
+            "bulk": lax.rem(bulk + (d // deep) * count, nb),
+            "group": lax.rem(group + 2 * (d % deep), ng),
+        }
+        for d in sorted(
+            range(1, across * deep), key=lambda d: -hops(d // deep, across) - hops(d % deep, deep)
+        )
     ]
 
 
@@ -141,9 +161,9 @@
     wnb_x,
     wnb_y,
     sum_send,
-    sum_group,
+    sum_plane,
     tot_send,
-    sum_bulk,
+    sum_cross,
     load_sem,
     res_ssem,
     res_rsem,
@@ -187,8 +207,15 @@
     barrier = pltpu.get_barrier_semaphore()
 
     near_group = [{"group": lax.rem(group + d, ng)} for d in far_first(ng)]
-    far_bulk = far_targets(nb, bulk)
-    for target in near_group + far_bulk:
+    plane = plane_targets(nb, bulk, group)
+    cross = cross_targets(nb, ng, bulk, group)
+    n_plane = len(plane) + 1
+    n_cross = len(cross) + 1
+    in_plane = lax.rem(bulk, along_y(nb)) * 2 + lax.rem(group, 2)
+    in_cross = (bulk // along_y(nb)) * (ng // 2) + group // 2
+    beside = [{"bulk": lax.rem(bulk + d, nb)} for d in (1, nb - 1)]
+    greeted = cross + near_group + plane + beside
+    for target in greeted:
         pl.semaphore_signal(barrier, inc=1, device_id=target, device_id_type=pl.DeviceIdType.MESH)
     for copy in small_loads + prec_loads + inv_loads + diag_loads:
         copy.start()
@@ -534,23 +561,25 @@
 
     def sum_start(n, payload):
         sum_send[n] = payload
-        sum_group[n, group] = payload
-        for target in near_group:
+        sum_plane[n, in_plane] = payload
+        for target in plane:
             remote(
-                sum_send.at[n], sum_group.at[n, group], g_ssem.at[n], g_rsem.at[n], target
+                sum_send.at[n], sum_plane.at[n, in_plane], g_ssem.at[n], g_rsem.at[n], target
             ).start()
 
     def sum_middle(n):
-        all_but_one(sum_group.at[n], ng, g_rsem.at[n]).wait()
-        partial = jnp.sum(sum_group[n], axis=0)
+        all_but_one(sum_plane.at[n], n_plane, g_rsem.at[n]).wait()
+        partial = jnp.sum(sum_plane[n], axis=0)
         tot_send[n] = partial
-        sum_bulk[n, bulk] = partial
-        for target in far_bulk:
-            remote(tot_send.at[n], sum_bulk.at[n, bulk], b_ssem.at[n], b_rsem.at[n], target).start()
+        sum_cross[n, in_cross] = partial
+        for target in cross:
+            remote(
+                tot_send.at[n], sum_cross.at[n, in_cross], b_ssem.at[n], b_rsem.at[n], target
+            ).start()
 
     def sum_finish(n, count):
-        all_but_one(sum_bulk.at[n], nb, b_rsem.at[n]).wait()
-        total = jnp.sum(sum_bulk[n], axis=0)
+        all_but_one(sum_cross.at[n], n_cross, b_rsem.at[n]).wait()
+        total = jnp.sum(sum_cross[n], axis=0)
         swapped = pltpu.roll(total, COLS, 1)
         low = low_half((4, LANES))
         halves = (jnp.where(low, total, swapped), jnp.where(low, swapped, total))
@@ -562,7 +591,7 @@
         return (factor * value.reshape(-1, 8, LANES)).reshape(value.shape)
 
     coarse_residual(0, k0)
-    pl.semaphore_wait(barrier, ng + nb - 2)
+    pl.semaphore_wait(barrier, len(greeted))
     coarse_push(0)
     weight_copies = edge_copies(wtab, wnb_x, wnb_y, ITERS)
     for copy in weight_copies:
@@ -713,11 +742,11 @@
             copy.wait_send()
     for step in range(ITERS):
         all_but_one(res_buf.at[step], ng, res_ssem.at[step]).wait()
-    all_but_one(sum_group.at[0], ng, g_ssem.at[0]).wait()
-    all_but_one(sum_bulk.at[0], nb, b_ssem.at[0]).wait()
+    all_but_one(sum_plane.at[0], n_plane, g_ssem.at[0]).wait()
+    all_but_one(sum_cross.at[0], n_cross, b_ssem.at[0]).wait()
 
     sum_middle(1)
-    all_but_one(sum_group.at[1], ng, g_ssem.at[1]).wait()
+    all_but_one(sum_plane.at[1], n_plane, g_ssem.at[1]).wait()
     d_11, d_0w, d_1w, d_ww, d_0v, d_1v, d_wv, d_vv = sum_finish(1, 8)
     d_01 = c1 * sum_kw * (tiny_eps * s0 * s0)
 
@@ -776,7 +805,7 @@
 
     loop(PAIRS, finish)
 
-    all_but_one(sum_bulk.at[1], nb, b_ssem.at[1]).wait()
+    all_but_one(sum_cross.at[1], n_cross, b_ssem.at[1]).wait()
 
 
 def body(nb, ng, rhs, diag_blocks, precond_blocks, coupling, face_open, agg_id, coarse_basis, coarse_inv):
@@ -823,9 +852,9 @@
             pltpu.VMEM((CX, HALF, 8, LANES), f32),
             pltpu.VMEM((CX, 2, 8, LANES), f32),
             pltpu.VMEM((2, 4, LANES), f32),
-            pltpu.VMEM((2, ng, 4, LANES), f32),
+            pltpu.VMEM((2, 2 * along_y(nb), 4, LANES), f32),
             pltpu.VMEM((2, 4, LANES), f32),
-            pltpu.VMEM((2, nb, 4, LANES), f32),
+            pltpu.VMEM((2, (nb // along_y(nb)) * (ng // 2), 4, LANES), f32),
             dma((14,)),
             dma((ITERS,)),
             dma((ITERS,)),

time: 55.8 us -> 54.2 us (0.971)
  Pallas kernels: 54.8 us -> 53.3 us
    pallas_call x1, Pallas kernels: 54.8 us -> 53.3 us  [body(): call(*[pltpu.with_memory_space_constraint(x, pltpu.HBM) for x in operands])]
where the time goes in v7:
time: 54.2 us; the launch traced here: 54.1 us
  Pallas kernels  53.3 us (98%)
  local copies, waits for them, and re-layouts  0.8 us (1%)
    pallas_call x1, Pallas kernels, body(): call(*[pltpu.with_memory_space_constraint(x, pltpu.HBM) for x in operands])  53.3 us

profile of v7, /device:TPU:1, one launch (start us, length us, event | category | flops | bytes accessed | tf_op | source)
XLA Modules:
  0.0 54.1 jit_solution(13494003458617824221)
XLA Ops:
  0.0 53.3 %shard_map.82 = bf16[2,16,64,64]{3,2,1,0:T(8,128)(2,1)S(1)} custom-call(bf16[2,16,64,64]{3,2,1,0:T(8,128)(2,1)} %rhs_hbm.1, bf16[2,16,64,64]{3,2,1,0:T(8,128)(2,1)} %diag_hbm.1, bf16[2,16,64,64]{3,2,1,0:T(8,128)(2,1)} %prec_hbm.1, f32[2,16,256]{2,1,0:T(8,128)} %coup_hbm.1, s32[2,4,16]{2,1,0:T(4,128)} %bitcast.6, s32[2,16]{1,0:T(2,128)} %agg_hbm.1, ...), custom_call_target="tpu_custom_call" | custom-call | flops 200000000 | bytes 3000000 | tf_op jit(solution)/shard_map/pallas_call | solution.py:887
  53.3 0.8 %copy.10 = bf16[2,16,64,64]{3,2,1,0:T(8,128)(2,1)} copy(bf16[2,16,64,64]{3,2,1,0:T(8,128)(2,1)S(1)} %shard_map.82) | data formatting | bytes 524288
